TPU v7x, 768 devices: a whole 4x8x12 slice. The times are simulated.
768 devices in a mesh: aux: 24 (over z_lo, x), orb: 4 (over z_hi, core), rep: 8 (over y).
Axes of the slice: x: 4, y: 8, z: 12 (z_hi: 2, z_lo: 6; z = z_hi * 6 + z_lo), core: 2. Of those that a mesh axis runs over, the one named last changes fastest.
Arguments:
- tiles: bfloat16 [24, 32, 8, 1600, 128], P('aux', ('orb', 'rep')), may hold values from -0.109375 to 0.109375
- atom_of: int32 [24, 32, 8], P('aux', ('orb', 'rep')), may hold values from 0 to 31
- owner_of: int32 [24, 32, 8], P('aux', ('orb', 'rep')), may hold values from 0 to 23
- live_count: int32 [24, 32], P('aux', ('orb', 'rep')), may hold values from 1 to 8, as said below
- green: bfloat16 [2, 1280, 1280], P(None, None, 'orb'), may hold values from -0.15625 to 0.15625
- probes: bfloat16 [12, 3072], P(None, 'aux'), may hold values from -6 to 6
Outputs:
- response: float32 [12, 3072], P(None, 'aux')
Inputs may be any that keep to these rules, and one draw needn't show every extreme that they name: `atom_of`: a block's orbital atom. `owner_of`: a block's auxiliary block. The first live_count slots of a list are its blocks, the rest are padding; some list is full.
All inputs are finite; a program needn't handle non-finite values.
Results may differ from a plain program's by a relative error of at most 0.0075.
Values may be sent and summed in bfloat16 or wider, within the bound.
No kernel may reach another device: no remote copies, remote signals or barrier semaphores. Data moves between devices by JAX's collectives and lax.ppermute only.
A program may use at most 64 MiB of HBM per device.

v0:
```python
import jax
import jax.numpy as jnp
from jax import lax
from jax.sharding import PartitionSpec as P

BO = 40
NPROBE = 12


def from_behind(value, axis, by):
    length = lax.axis_size(axis)
    return lax.ppermute(value, axis, [(i, (i + by) % length) for i in range(length)])


def body(tiles, atom_of, owner_of, live_count, green, probes):
    blocks = tiles[0, 0]
    lam_atoms = atom_of[0, 0]
    owners = owner_of[0, 0]
    live_total = live_count[0, 0]
    slot_count = blocks.shape[0]
    aux_width = blocks.shape[2]
    orb_total = green.shape[1]
    panel_width = green.shape[2]
    aux_groups = lax.axis_size("aux")
    orb_count = lax.axis_size("orb")
    orb_place = lax.axis_index("orb")
    everyone = lax.all_gather(probes, "aux", axis=1, tiled=True)
    live_mask = (jnp.arange(slot_count) < live_total).astype(jnp.float32)
    chosen = jnp.take(everyone.reshape(NPROBE, aux_groups, aux_width), owners, axis=1)
    contracted = jnp.einsum("rbq,bkq->brk", chosen, blocks, preferred_element_type=jnp.float32)
    contracted = (contracted * live_mask[:, None, None]).astype(jnp.bfloat16)
    stacked = jnp.transpose(contracted.reshape(slot_count, NPROBE, BO, BO), (1, 2, 0, 3))
    stacked = stacked.reshape(NPROBE * BO, slot_count * BO)
    rows_index = (lam_atoms[:, None] * BO + jnp.arange(BO, dtype=jnp.int32)[None, :]).reshape(-1)
    w_field = jnp.zeros((NPROBE * BO, orb_total), jnp.float32)
    v_field = jnp.zeros((NPROBE * BO, slot_count * BO), jnp.float32)
    green_panel = green[1]
    for turn_index in range(orb_count):
        add_selected = jnp.take(green_panel, rows_index, axis=0)
        columns = jnp.dot(stacked, add_selected, preferred_element_type=jnp.float32)
        w_field = lax.dynamic_update_slice_in_dim(
            w_field, columns, (orb_place - turn_index) % orb_count * panel_width, 1
        )
        if turn_index + 1 < orb_count:
            green_panel = from_behind(green_panel, "orb", 1)
    w_half = lax.psum(w_field, "aux").astype(jnp.bfloat16)
    green_panel = green[0]
    for turn_index in range(orb_count):
        selected = jnp.take(green_panel, rows_index, axis=0)
        w_part = lax.dynamic_slice_in_dim(
            w_half, (orb_place - turn_index) % orb_count * panel_width, panel_width, 1
        )
        v_field = v_field + lax.dot_general(
            w_part, selected, (((1,), (1,)), ((), ())), preferred_element_type=jnp.float32
        )
        if turn_index + 1 < orb_count:
            green_panel = from_behind(green_panel, "orb", 1)
    v_half = v_field.astype(jnp.bfloat16)
    picked = jnp.transpose(v_half.reshape(NPROBE, BO, slot_count, BO), (2, 0, 1, 3))
    picked = picked.reshape(slot_count, NPROBE, BO * BO)
    y_rows = jnp.einsum("brk,bkp->brp", picked, blocks, preferred_element_type=jnp.float32)
    y_rows = y_rows * live_mask[:, None, None]
    owner_hot = (owners[:, None] == jnp.arange(aux_groups, dtype=jnp.int32)[None, :]).astype(
        jnp.float32
    )
    sending = jnp.einsum("bc,brp->rcp", owner_hot, y_rows).reshape(NPROBE, aux_groups * aux_width)
    summed = lax.psum(sending, ("aux", "orb", "rep"))
    result = lax.dynamic_slice_in_dim(summed, lax.axis_index("aux") * aux_width, aux_width, 1)
    return result


def solution(mesh):
    return jax.shard_map(
        body,
        mesh=mesh,
        in_specs=(
            P("aux", ("orb", "rep"), None, None, None),
            P("aux", ("orb", "rep"), None),
            P("aux", ("orb", "rep"), None),
            P("aux", ("orb", "rep")),
            P(None, None, "orb"),
            P(None, "aux"),
        ),
        out_specs=P(None, "aux"),
        check_vma=False,
    )
```

profile of v0, /device:TPU:1, one launch (start us, length us, event | category | flops | bytes accessed | tf_op | source)
XLA Modules:
  0.0 904.6 jit_solution(11770620351681817712)
XLA Ops:
  6.6 3.1 slice_bitcast_fusion
  9.7 16.2 %collective-permute-start = (bf16[1280,320]{0,1:T(8,128)(2,1)S(1)}, bf16[1280,320]{0,1:T(8,128)(2,1)}, u32[]{:S(2)}, u32[]{:S(2)}) collective-permute-start(bf16[1280,320]{0,1:T(8,128)(2,1)S(1)} %get-tuple-element.7), channel_id=1, source_target_pairs={{0,8},{8,16},{16,24},{24,0},{1,9},{9,17},{17,25},{25,1},{2,10},{10... | collective-permute-start | bytes 2457608 | tf_op jit(solution)/shard_map/ppermute | solution.py:12
  25.9 1.9 collective-permute-start.3
  28.6 19.5 %collective-permute-done = bf16[1280,320]{0,1:T(8,128)(2,1)} collective-permute-done((bf16[1280,320]{0,1:T(8,128)(2,1)S(1)}, bf16[1280,320]{0,1:T(8,128)(2,1)}, u32[]{:S(2)}, u32[]{:S(2)}) %collective-permute-start) | collective-permute-done | bytes 819232 | tf_op jit(solution)/shard_map/ppermute | solution.py:12
  48.1 11.0 %collective-permute-start.1 = (bf16[1280,320]{0,1:T(8,128)(2,1)}, bf16[1280,320]{0,1:T(8,128)(2,1)}, u32[]{:S(2)}, u32[]{:S(2)}) collective-permute-start(bf16[1280,320]{0,1:T(8,128)(2,1)} %collective-permute-done), channel_id=1, source_target_pairs={{0,8},{8,16},{16,24},{24,0},{1,9},{9,17},{17,25},{25,1},{2,10},{10... | collective-permute-start | bytes 2457608 | tf_op jit(solution)/shard_map/ppermute | solution.py:12
  59.3 113.5 %all_gather.3 = bf16[12,3072]{1,0:T(8,128)(2,1)S(1)} all-gather(bf16[12,128]{1,0:T(8,128)(2,1)S(1)} %copy-done.5), channel_id=1, replica_groups=mesh['aux'=24,'orb'=4,'rep'=8] {'aux'}, dimensions={1}, use_global_device_ids=true | all-gather | bytes 76800 | tf_op jit(solution)/shard_map/all_gather | solution.py:27
  172.8 0.6 gather_fusion
  173.4 1.8 fusion.7
  175.3 1.9 collective-permute-start.4
  177.2 1.9 collective-permute-start.2
  179.2 2.2 copy.44
  181.4 1.8 copy.25
  183.2 2.7 reshape.77
  185.9 2.4 copy.26
  188.3 2.6 reshape.78
  190.9 2.2 copy.43
  193.1 3.2 gather_fusion.1
  196.3 3.7 gather_fusion.5
  200.0 1.8 broadcast_in_dim.26
  201.9 1.4 convolution_dynamic-update-slice_fusion.3
  203.2 2.2 copy.29
  205.5 3.7 gather_fusion.2
  209.2 2.2 copy.34
  211.4 3.2 gather_fusion.6
  214.6 2.4 convolution_dynamic-update-slice_fusion.2
  217.1 2.2 copy.30
  219.3 3.7 gather_fusion.3
  223.0 2.2 copy.35
  225.2 3.7 gather_fusion.7
  228.9 10.6 %collective-permute-start.5 = (bf16[1280,320]{0,1:T(8,128)(2,1)}, bf16[1280,320]{0,1:T(8,128)(2,1)}, u32[]{:S(2)}, u32[]{:S(2)}) collective-permute-start(bf16[1280,320]{0,1:T(8,128)(2,1)} %collective-permute-done.4), channel_id=1, source_target_pairs={{0,8},{8,16},{16,24},{24,0},{1,9},{9,17},{17,25},{25,1},{2,10},{10... | collective-permute-start | bytes 2457608 | tf_op jit(solution)/shard_map/ppermute | solution.py:12
  239.5 2.4 convolution_dynamic-update-slice_fusion.1
  241.9 2.2 copy.31
  244.2 3.7 gather_fusion.4
  247.9 2.4 convolution_dynamic-update-slice_fusion
  250.3 152.7 %all-reduce.4 = bf16[480,1280]{0,1:T(8,128)(2,1)} all-reduce(f32[480,1280]{0,1:T(8,128)} %convolution_dynamic-update-slice_fusion), channel_id=1, replica_groups=mesh['aux'=24,'orb'=4,'rep'=8] {'aux'}, use_global_device_ids=true, to_apply=%region_0.0 | all-reduce | flops 614400 | bytes 3686400 | tf_op jit(solution)/shard_map/psum | solution.py:46
  402.9 2.2 copy.36
  405.1 3.7 gather_fusion.8
  408.9 1.6 fusion.17
  410.5 1.4 convolution_add_fusion.2
  412.2 1.1 fusion.10
  413.3 1.9 copy.37
  415.3 2.6 reshape.79
  417.9 2.3 copy.41
  420.2 2.7 reshape.179
  422.9 1.6 fusion.11
  424.8 0.7 copy.48
  425.5 471.0 %all-reduce.3.cloned.1.call-done = f32[12,3072]{1,0:T(8,128)} async-done(((f32[12,3072]{1,0:T(8,128)}), f32[12,3072]{1,0:T(8,128)}) %all-reduce.3.cloned.1.call-update) | async-done | bytes 147472 | tf_op jit(solution)/shard_map/psum | solution.py:67
  896.5 1.3 constant_dynamic-slice_fusion
  (38 shorter events, 1.0 us)
Async XLA Ops:
  6.5 166.9 %copy-start = (bf16[1,1,8,1600,128]{4,3,2,1,0:T(8,128)(2,1)S(1)}, bf16[1,1,8,1600,128]{4,3,2,1,0:T(8,128)(2,1)}, u32[]{:S(2)}) copy-start(bf16[1,1,8,1600,128]{4,3,2,1,0:T(8,128)(2,1)} %param.8) | copy-start | bytes 9830404
  6.5 22.0 %copy-start.7 = (s32[1,1,8]{2,1,0:T(1,128)S(1)}, s32[1,1,8]{2,1,0:T(1,128)}, u32[]{:S(2)}) copy-start(s32[1,1,8]{2,1,0:T(1,128)} %param.9) | copy-start | bytes 100
  6.5 22.0 %copy-start.6 = (s32[1,1,8]{2,1,0:T(1,128)S(1)}, s32[1,1,8]{2,1,0:T(1,128)}, u32[]{:S(2)}) copy-start(s32[1,1,8]{2,1,0:T(1,128)} %param.10) | copy-start | bytes 100
  6.5 52.7 %copy-start.5 = (bf16[12,128]{1,0:T(8,128)(2,1)S(1)}, bf16[12,128]{1,0:T(8,128)(2,1)}, u32[]{:S(2)}) copy-start(bf16[12,128]{1,0:T(8,128)(2,1)} %param.13) | copy-start | bytes 9220
  6.5 890.0 %all-reduce.3.cloned.1.call-start = ((), (), s32[]{:S(2)}) async-start(), calls=%async_computation | async-start | bytes 393216 | tf_op jit(solution)/shard_map/psum | solution.py:67
  9.7 38.4 %collective-permute-start = (bf16[1280,320]{0,1:T(8,128)(2,1)S(1)}, bf16[1280,320]{0,1:T(8,128)(2,1)}, u32[]{:S(2)}, u32[]{:S(2)}) collective-permute-start(bf16[1280,320]{0,1:T(8,128)(2,1)S(1)} %get-tuple-element.7), channel_id=1, source_target_pairs={{0,8},{8,16},{16,24},{24,0},{1,9},{9,17},{17,25},{25,1},{2,10},{10... | collective-permute-start | bytes 2457608 | tf_op jit(solution)/shard_map/ppermute | solution.py:12
  25.9 149.3 %collective-permute-start.3 = (bf16[1280,320]{0,1:T(8,128)(2,1)}, bf16[1280,320]{0,1:T(8,128)(2,1)}, u32[]{:S(2)}, u32[]{:S(2)}) collective-permute-start(bf16[1280,320]{0,1:T(8,128)(2,1)} %get-tuple-element.6), channel_id=1, source_target_pairs={{0,8},{8,16},{16,24},{24,0},{1,9},{9,17},{17,25},{25,1},{2,10},{10... | collective-permute-start | bytes 2457608 | tf_op jit(solution)/shard_map/ppermute | solution.py:12
  48.1 129.1 %collective-permute-start.1 = (bf16[1280,320]{0,1:T(8,128)(2,1)}, bf16[1280,320]{0,1:T(8,128)(2,1)}, u32[]{:S(2)}, u32[]{:S(2)}) collective-permute-start(bf16[1280,320]{0,1:T(8,128)(2,1)} %collective-permute-done), channel_id=1, source_target_pairs={{0,8},{8,16},{16,24},{24,0},{1,9},{9,17},{17,25},{25,1},{2,10},{10... | collective-permute-start | bytes 2457608 | tf_op jit(solution)/shard_map/ppermute | solution.py:12
  175.3 47.7 %collective-permute-start.4 = (bf16[1280,320]{0,1:T(8,128)(2,1)}, bf16[1280,320]{0,1:T(8,128)(2,1)}, u32[]{:S(2)}, u32[]{:S(2)}) collective-permute-start(bf16[1280,320]{0,1:T(8,128)(2,1)} %collective-permute-done.3), channel_id=1, source_target_pairs={{0,8},{8,16},{16,24},{24,0},{1,9},{9,17},{17,25},{25,1},{2,10},{10... | collective-permute-start | bytes 2457608 | tf_op jit(solution)/shard_map/ppermute | solution.py:12
  177.2 64.7 %collective-permute-start.2 = (bf16[1280,320]{0,1:T(8,128)(2,1)}, bf16[1280,320]{0,1:T(8,128)(2,1)}, u32[]{:S(2)}, u32[]{:S(2)}) collective-permute-start(bf16[1280,320]{0,1:T(8,128)(2,1)} %collective-permute-done.1), channel_id=1, source_target_pairs={{0,8},{8,16},{16,24},{24,0},{1,9},{9,17},{17,25},{25,1},{2,10},{10... | collective-permute-start | bytes 2457608 | tf_op jit(solution)/shard_map/ppermute | solution.py:12
  200.0 1.8 copy-start.1
  228.9 174.0 %collective-permute-start.5 = (bf16[1280,320]{0,1:T(8,128)(2,1)}, bf16[1280,320]{0,1:T(8,128)(2,1)}, u32[]{:S(2)}, u32[]{:S(2)}) collective-permute-start(bf16[1280,320]{0,1:T(8,128)(2,1)} %collective-permute-done.4), channel_id=1, source_target_pairs={{0,8},{8,16},{16,24},{24,0},{1,9},{9,17},{17,25},{25,1},{2,10},{10... | collective-permute-start | bytes 2457608 | tf_op jit(solution)/shard_map/ppermute | solution.py:12
  408.8 3.0 copy-start.2
  408.8 3.0 copy-start.3
  408.8 3.4 copy-start.4
Sparse Core Ops, SparseCore 0:
  425.6 470.8 all-reduce.2
where the time goes:
time: 907 us; the launch traced here: 905 us
  waiting for transfers between devices  490 us (54%)
  blocking collectives  266 us (29%)
  local copies, waits for them, and re-layouts  73.1 us (8%)
  starting transfers between devices  43.7 us (5%)
  matrix products  16.7 us (2%)
  between operations  14.4 us (2%)
    psum x1, waiting for transfers between devices, body(): summed = lax.psum(sending, ('aux', 'orb', 'rep'))  471 us
    psum x1, blocking collectives, body(): w_half = lax.psum(w_field, 'aux').astype(jnp.bfloat16)  153 us
    all_gather x1, blocking collectives, body(): everyone = lax.all_gather(probes, 'aux', axis=1, tiled=True)  114 us
    ppermute x6, starting transfers between devices, from_behind(): lax.ppermute(value, axis, [(i, (i + by) % length) for i in range(length)])  43.6 us
    ppermute x6, waiting for transfers between devices, from_behind(): lax.ppermute(value, axis, [(i, (i + by) % length) for i in range(length)])  19.5 us
  transfers between devices with their start and end apart: 7, of which 2 were waited for; matrix products, arithmetic and copies ran while one was open for 7% of the time, Pallas kernels for 0%

commit v1 on v0

v1 whole, which is shorter than its diff:
```python
import functools

import jax
import jax.numpy as jnp
from jax import lax
from jax.experimental import pallas as pl
from jax.experimental.pallas import tpu as pltpu
from jax.sharding import Mesh
from jax.sharding import PartitionSpec as P

BO = 40
NPROBE = 12
HALVES = 2
SIG = BO // HALVES
LANE = 128
F32 = jnp.float32
BF16 = jnp.bfloat16

Z_HI = 2
AUX = ("z_lo", "x")
OUTER = ("z_hi", "z_lo", "x")
REST = ("z_hi", "core", "rep")


def iota(shape, dim):
    return lax.broadcasted_iota(jnp.int32, shape, dim)


def dot(a, b, ca, cb):
    return lax.dot_general(a, b, (((ca,), (cb,)), ((), ())), preferred_element_type=F32)


def u_kernel(owners_ref, atoms_ref, live_ref, probes_ref, tiles_ref, out_ref, acc_ref):
    b = pl.program_id(0)
    slots = pl.num_programs(0)
    slot_count = out_ref.shape[2]
    width = SIG * BO

    chosen = probes_ref[owners_ref[b]].astype(F32)
    rows = jnp.broadcast_to(chosen[:, None, :], (NPROBE, slot_count, chosen.shape[1]))
    keep = (iota(rows.shape, 1) == b) & (b < live_ref[0])
    rows = jnp.where(keep, rows, 0.0).reshape(NPROBE * slot_count, chosen.shape[1]).astype(BF16)
    part = dot(rows, tiles_ref[0], 1, 1)

    @pl.when(b == 0)
    def _():
        acc_ref[...] = part

    @pl.when(b > 0)
    def _():
        acc_ref[...] += part

    @pl.when(b == slots - 1)
    def _():
        tail = out_ref.shape[3] - width
        ids = jnp.zeros((slot_count, tail), F32)
        for k in range(slot_count):
            ids = jnp.where(iota(ids.shape, 0) == k, atoms_ref[k].astype(F32), ids)
        ids = jnp.broadcast_to(ids[None], (NPROBE, slot_count, tail)).astype(BF16)
        for h in range(HALVES):
            piece = acc_ref[:, h * width : (h + 1) * width]
            piece = piece.reshape(NPROBE, slot_count, width).astype(BF16)
            for z in range(Z_HI):
                out_ref[z, h * NPROBE : (h + 1) * NPROBE, :, :width] = piece
                out_ref[z, h * NPROBE : (h + 1) * NPROBE, :, width:] = ids


def make_u(tiles, probes_all, owners, atoms, live):
    slot_count, inner, aux_width = tiles.shape
    chunks = NPROBE * HALVES
    wide = -(-(SIG * BO + 1) // LANE) * LANE
    smem = pl.BlockSpec(memory_space=pltpu.SMEM)
    return pl.pallas_call(
        u_kernel,
        grid=(slot_count,),
        in_specs=[
            smem,
            smem,
            smem,
            pl.BlockSpec(probes_all.shape, lambda b: (0, 0, 0)),
            pl.BlockSpec((1, inner, aux_width), lambda b: (b, 0, 0)),
        ],
        out_specs=pl.BlockSpec((Z_HI, chunks, slot_count, wide), lambda b: (0, 0, 0, 0)),
        out_shape=jax.ShapeDtypeStruct((Z_HI, chunks, slot_count, wide), BF16),
        scratch_shapes=[pltpu.VMEM((NPROBE * slot_count, inner), F32)],
        compiler_params=pltpu.CompilerParams(vmem_limit_bytes=32 * 2**20),
        name="u_blocks",
    )(owners, atoms, live, probes_all, tiles)


def w_kernel(recv_ref, mine_ref, other_ref, out_ref):
    senders, slot_count, _ = recv_ref.shape
    half = senders // Z_HI
    queue = half * slot_count
    orb = mine_ref.shape[1]
    atoms = orb // BO
    width = SIG * BO

    copies = (iota((BO, orb), 1) % BO == iota((BO, orb), 0)).astype(BF16)
    own_atom = iota((atoms, orb), 1) // BO == iota((atoms, orb), 0)

    hots, spreads = [], []
    for z in range(Z_HI):
        got = recv_ref[z * half : (z + 1) * half].astype(F32).reshape(queue, recv_ref.shape[2])
        ids = got[:, width : width + 1].astype(jnp.int32)
        hot = (iota((queue, atoms), 1) == ids).astype(BF16)
        hots.append(hot)
        spread = dot(hot, got[:, :width].astype(BF16), 0, 0)
        spreads += [spread[:, s * BO : (s + 1) * BO] for s in range(SIG)]
    stacked = jnp.concatenate(spreads, axis=0)
    high = stacked.astype(BF16)
    low = (stacked - high.astype(F32)).astype(BF16)
    count = Z_HI * SIG

    def by_row(part):
        full = dot(part, copies, 1, 0).reshape(count, atoms, orb)
        return jnp.sum(jnp.where(own_atom[None], full, 0.0), axis=1).astype(BF16)

    high, low = by_row(high), by_row(low)
    v = None
    for panel in (mine_ref, other_ref):
        w = dot(high, panel[1], 1, 0) + dot(low, panel[1], 1, 0)
        part = dot(w.astype(BF16), panel[0], 1, 1)
        v = part if v is None else v + part
    spread_v = jnp.where(own_atom[None], v[:, None, :], 0.0).reshape(count * atoms, orb).astype(BF16)
    spread_v = dot(spread_v, copies, 1, 1)
    for z in range(Z_HI):
        first = z * SIG * atoms
        pieces = [spread_v[first + s * atoms : first + (s + 1) * atoms] for s in range(SIG)]
        table = jnp.concatenate(pieces, axis=1).astype(BF16)
        back = dot(hots[z], table, 1, 0).reshape(half, slot_count, width)
        out_ref[z * half : (z + 1) * half] = back.astype(BF16)


def make_v(recv, mine, other):
    senders, slot_count, _ = recv.shape
    return pl.pallas_call(
        w_kernel,
        out_shape=jax.ShapeDtypeStruct((senders, slot_count, SIG * BO), BF16),
        compiler_params=pltpu.CompilerParams(vmem_limit_bytes=56 * 2**20),
        name="w_and_v",
    )(recv, mine, other)


def y_kernel(owners_ref, live_ref, v_ref, tiles_ref, out_ref, lhs_ref):
    b = pl.program_id(0)
    slot_count = v_ref.shape[2]
    width = v_ref.shape[3]
    rows = NPROBE * slot_count

    @pl.when(b == 0)
    def _():
        out_ref[...] = jnp.zeros_like(out_ref)
        for h in range(HALVES):
            block = pl.ds(h * NPROBE, NPROBE)
            total = v_ref[0, block].astype(F32)
            for z in range(1, Z_HI):
                total = total + v_ref[z, block].astype(F32)
            lhs_ref[h] = total.reshape(rows, width).astype(BF16)

    @pl.when(b < live_ref[0])
    def _():
        y = None
        for h in range(HALVES):
            part = dot(lhs_ref[h], tiles_ref[0, h * width : (h + 1) * width, :], 1, 0)
            y = part if y is None else y + part
        y = y.reshape(NPROBE, slot_count, y.shape[1])
        y = jnp.sum(jnp.where(iota(y.shape, 1) == b, y, 0.0), axis=1)
        out_ref[owners_ref[b]] += y


def make_y(v, tiles, owners, live, groups):
    slot_count, inner, aux_width = tiles.shape
    smem = pl.BlockSpec(memory_space=pltpu.SMEM)
    return pl.pallas_call(
        y_kernel,
        grid=(slot_count,),
        in_specs=[
            smem,
            smem,
            pl.BlockSpec(v.shape, lambda b: (0, 0, 0, 0)),
            pl.BlockSpec((1, inner, aux_width), lambda b: (b, 0, 0)),
        ],
        out_specs=pl.BlockSpec((groups, NPROBE, aux_width), lambda b: (0, 0, 0)),
        out_shape=jax.ShapeDtypeStruct((groups, NPROBE, aux_width), F32),
        scratch_shapes=[pltpu.VMEM((HALVES, NPROBE * slot_count, v.shape[3]), BF16)],
        compiler_params=pltpu.CompilerParams(vmem_limit_bytes=32 * 2**20),
        name="y_by_owner",
    )(owners, live, v, tiles)


def everywhere(value, axes):
    count = lax.axis_size(axes)
    copies = jnp.broadcast_to(value[None], (count,) + value.shape)
    return lax.all_to_all(copies, axes, 0, 0)


def body(tiles, atom_of, owner_of, live_count, green, probes):
    tiles, atoms, owners, live = tiles[0, 0], atom_of[0, 0], owner_of[0, 0], live_count[0]
    slot_count = tiles.shape[0]
    groups = lax.axis_size(AUX)
    other = lax.ppermute(green, "core", [(0, 1), (1, 0)])
    probes_all = everywhere(probes, AUX)
    u = make_u(tiles, probes_all, owners, atoms, live)
    u = u.reshape((Z_HI * groups,) + u.shape[2:])
    recv = lax.all_to_all(u, OUTER, 0, 0)
    v = make_v(recv, green, other)
    v = lax.all_to_all(v, OUTER, 0, 0)
    v = v.reshape(Z_HI, groups, slot_count, SIG * BO)
    y = make_y(v, tiles, owners, live, groups)
    y = lax.all_to_all(y, AUX, 0, 0)
    y = jnp.sum(y, axis=0)
    return jnp.sum(everywhere(y, REST), axis=0)


def solution(mesh):
    aux, orb, rep = mesh.devices.shape
    x = 4
    fine = Mesh(mesh.devices.reshape(aux // x, x, Z_HI, orb // Z_HI, rep), ("z_lo", "x", "z_hi", "core", "rep"))
    orbs = ("z_hi", "core")
    return jax.shard_map(
        body,
        mesh=fine,
        in_specs=(
            P(AUX, orbs + ("rep",), None, None, None),
            P(AUX, orbs + ("rep",), None),
            P(AUX, orbs + ("rep",), None),
            P(AUX, orbs + ("rep",)),
            P(None, None, orbs),
            P(None, AUX),
        ),
        out_specs=P(None, AUX),
        check_vma=False,
    )
```

time: 907 us -> 172 us (0.19)
  waiting for transfers between devices: 490 us -> 27.9 us
  blocking collectives: 266 us -> 82.4 us
  local copies, waits for them, and re-layouts: 73.1 us -> 11.5 us
  matrix products: 16.7 us -> 0 us
  Pallas kernels: 0 us -> 16 us
  starting transfers between devices: 43.7 us -> 29.9 us
  between operations: 14.4 us -> 0.7 us
    psum x1 -> x0, waiting for transfers between devices: 471 us -> none  [body(): summed = lax.psum(sending, ('aux', 'orb', 'rep'))]
    psum x1 -> x0, blocking collectives: 153 us -> none  [body(): w_half = lax.psum(w_field, 'aux').astype(jnp.bfloat16)]
    all_gather x1 -> x0, blocking collectives: 114 us -> none  [body(): everyone = lax.all_gather(probes, 'aux', axis=1, tiled=True)]
    all_to_all x0 -> x3, blocking collectives: none -> 82.4 us  [the longest x1 34.8 us: body(): v = lax.all_to_all(v, OUTER, 0, 0)]
    ppermute x6 -> x1, starting transfers between devices: 43.6 us -> 4.26 us  [body(): other = lax.ppermute(green, 'core', [(0, 1), (1, 0)])]
    gather x9 -> x0, local copies, waits for them, and re-layouts: 29.3 us -> none  [the longest x4 14.4 us: body(): selected = jnp.take(green_panel, rows_index, axis=0)]
    all_to_all x0 -> x2, waiting for transfers between devices: none -> 27 us  [the longest x1 17.5 us: body(): recv = lax.all_to_all(u, OUTER, 0, 0)]
    all_to_all x0 -> x2, starting transfers between devices: none -> 25.7 us  [the longest x1 15.4 us: everywhere(): return lax.all_to_all(copies, axes, 0, 0)]
  transfers between devices with their start and end apart: 7 -> 3, of which waited for: 2 -> 3; matrix products, arithmetic and copies ran while one was open for 7% -> 4% of each run, Pallas kernels for 0% -> 0%
where the time goes in v1:
time: 172 us; the launch traced here: 169 us
  blocking collectives  82.4 us (48%)
  starting transfers between devices  29.9 us (17%)
  waiting for transfers between devices  27.9 us (16%)
  Pallas kernels  16 us (9%)
  local copies, waits for them, and re-layouts  11.5 us (7%)
    all_to_all x1, blocking collectives, body(): v = lax.all_to_all(v, OUTER, 0, 0)  34.8 us
    all_to_all x1, blocking collectives, everywhere(): return lax.all_to_all(copies, axes, 0, 0)  32.8 us
    all_to_all x1, waiting for transfers between devices, body(): recv = lax.all_to_all(u, OUTER, 0, 0)  17.5 us
    all_to_all x1, starting transfers between devices, everywhere(): return lax.all_to_all(copies, axes, 0, 0)  15.4 us
    all_to_all x1, blocking collectives, body(): y = lax.all_to_all(y, AUX, 0, 0)  14.9 us
    all_to_all x1, starting transfers between devices, body(): recv = lax.all_to_all(u, OUTER, 0, 0)  10.3 us
    pallas_call x1, Pallas kernels, make_v(): pl.pallas_call(w_kernel, out_shape=jax.ShapeDtypeStruct((senders, slot_co...  9.56 us
    all_to_all x1, waiting for transfers between devices, everywhere(): return lax.all_to_all(copies, axes, 0, 0)  9.54 us
  transfers between devices with their start and end apart: 3, of which 3 were waited for; matrix products, arithmetic and copies ran while one was open for 4% of the time, Pallas kernels for 0%

profile of v1, /device:TPU:1, one launch (start us, length us, event | category | flops | bytes accessed | tf_op | source)
XLA Modules:
  0.0 169.1 jit_solution(11180443350937339497)
XLA Ops:
  0.0 1.3 broadcast_in_dim.4
  1.3 15.4 %all-to-all-start = ((bf16[24,12,128]{2,1,0:T(8,128)(2,1)}), bf16[24,12,128]{2,1,0:T(8,128)(2,1)S(1)}, u32[]{:S(2)}, u32[]{:S(2)}) async-start(bf16[24,12,128]{2,1,0:T(8,128)(2,1)} %broadcast_in_dim.4), calls=%async_computation | async-start | bytes 196608 | tf_op jit(solution)/shard_map/all_to_all | solution.py:195
  17.3 9.5 %all-to-all-done.probes_ref = bf16[24,12,128]{2,1,0:T(8,128)(2,1)S(1)} async-done(((bf16[24,12,128]{2,1,0:T(8,128)(2,1)}), bf16[24,12,128]{2,1,0:T(8,128)(2,1)S(1)}, u32[]{:S(2)}, u32[]{:S(2)}) %all-to-all-start) | async-done | bytes 73760 | tf_op jit(solution)/shard_map/all_to_all | solution.py:195
  26.9 0.0 copy-start
  26.9 1.9 %copy-done = bf16[1,1,8,1600,128]{4,3,2,1,0:T(8,128)(2,1)S(1)} copy-done((bf16[1,1,8,1600,128]{4,3,2,1,0:T(8,128)(2,1)S(1)}, bf16[1,1,8,1600,128]{4,3,2,1,0:T(8,128)(2,1)}, u32[]{:S(2)}) %copy-start) | copy-done | bytes 3276824
  28.8 0.0 copy-start.2
  28.8 0.7 copy-done.2
  29.5 0.0 copy-start.4
  29.5 0.7 copy-done.4
  30.1 0.0 copy-start.6
  30.1 4.3 %u_blocks.1 = bf16[2,24,8,896]{3,2,1,0:T(8,128)(2,1)} custom-call(s32[8]{0:T(128)S(1)} %bitcast.11, s32[8]{0:T(128)S(1)} %bitcast.13, s32[1]{0:T(128)} %bitcast.6.live_ref, bf16[24,12,128]{2,1,0:T(8,128)(2,1)S(1)} %all-to-all-done.probes_ref, bf16[8,1600,128]{2,1,0:T(8,128)(2,1)S(1)} %bitcast.8), custom_call_target="tpu_custom_call" | custom-call | tf_op jit(solution)/shard_map/u_blocks/pallas_call | solution.py:73
  34.4 10.3 %all-to-all-start.1 = ((bf16[48,8,896]{2,1,0:T(8,128)(2,1)}), bf16[48,8,896]{2,1,0:T(8,128)(2,1)S(1)}, u32[]{:S(2)}, u32[]{:S(2)}) async-start(bf16[48,8,896]{2,1,0:T(8,128)(2,1)} %bitcast.4), calls=%async_computation.1 | async-start | bytes 1376256 | tf_op jit(solution)/shard_map/all_to_all | solution.py:206
  44.8 0.0 copy-done.6
  44.8 4.3 %collective-permute-start = (bf16[2,1280,320]{1,2,0:T(8,128)(2,1)S(1)}, bf16[2,1280,320]{1,2,0:T(8,128)(2,1)}, u32[]{:S(2)}, u32[]{:S(2)}) collective-permute-start(bf16[2,1280,320]{1,2,0:T(8,128)(2,1)S(1)} %copy-done.6), channel_id=1, source_target_pairs={{0,8},{8,0},{1,9},{9,1},{2,10},{10,2},{3,11},{11,3},{4,12},{12,4},... | collective-permute-start | bytes 4915208 | tf_op jit(solution)/shard_map/ppermute | solution.py:202
  49.0 2.4 %copy.13.mine_ref = bf16[2,1280,320]{2,1,0:T(8,128)(2,1)} copy(bf16[2,1280,320]{1,2,0:T(8,128)(2,1)S(1)} %copy-done.6) | data formatting | bytes 3276800 | tf_op args[4]
  51.4 0.8 collective-permute-done
  52.3 3.7 %copy.14.other_ref = bf16[2,1280,320]{2,1,0:T(8,128)(2,1)} copy(bf16[2,1280,320]{1,2,0:T(8,128)(2,1)} %collective-permute-done) | data formatting | bytes 3276800 | tf_op jit(solution)/shard_map/ppermute | solution.py:202
  55.9 0.0 copy-start.3
  56.0 17.5 %all-to-all-done.1.recv_ref = bf16[48,8,896]{2,1,0:T(8,128)(2,1)S(1)} async-done(((bf16[48,8,896]{2,1,0:T(8,128)(2,1)}), bf16[48,8,896]{2,1,0:T(8,128)(2,1)S(1)}, u32[]{:S(2)}, u32[]{:S(2)}) %all-to-all-start.1) | async-done | bytes 688160 | tf_op jit(solution)/shard_map/all_to_all | solution.py:206
  73.4 0.0 copy-start.5
  73.4 0.8 copy-done.5
  74.3 0.0 copy-start.1
  74.3 9.6 %w_and_v.1 = bf16[48,8,800]{2,1,0:T(8,128)(2,1)} custom-call(bf16[48,8,896]{2,1,0:T(8,128)(2,1)} %copy-done.5, bf16[2,1280,320]{2,1,0:T(8,128)(2,1)} %copy.13.mine_ref, bf16[2,1280,320]{2,1,0:T(8,128)(2,1)} %copy.14.other_ref), custom_call_target="tpu_custom_call" | custom-call | tf_op jit(solution)/shard_map/w_and_v/pallas_call | solution.py:137
  83.9 34.8 %all_to_all.25 = bf16[48,8,800]{2,1,0:T(8,128)(2,1)S(1)} all-to-all(bf16[48,8,800]{2,1,0:T(8,128)(2,1)} %w_and_v.1), channel_id=1, replica_groups=mesh['z_lo'=6,'x'=4,'z_hi'=2,'core'=2,'rep'=8] {'z_hi','z_lo','x'}, dimensions={0} | all-to-all | bytes 1228800 | tf_op jit(solution)/shard_map/all_to_all | solution.py:208
  118.6 0.0 copy-done.3
  118.7 0.0 copy-done.1
  118.7 2.1 %y_by_owner.1 = f32[24,12,128]{2,1,0:T(8,128)S(1)} custom-call(s32[8]{0:T(128)S(1)} %bitcast.12, s32[1]{0:T(128)} %bitcast.7.live_ref, bf16[2,24,8,800]{3,2,1,0:T(8,128)(2,1)S(1)} %bitcast.10, bf16[8,1600,128]{2,1,0:T(8,128)(2,1)S(1)} %bitcast.9), custom_call_target="tpu_custom_call" | custom-call | tf_op jit(solution)/shard_map/y_by_owner/pallas_call | solution.py:175
  120.8 14.9 %all_to_all.26 = f32[24,12,128]{2,1,0:T(8,128)S(1)} all-to-all(f32[24,12,128]{2,1,0:T(8,128)S(1)} %y_by_owner.1), channel_id=1, replica_groups=mesh['z_lo'=6,'x'=4,'z_hi'=2,'core'=2,'rep'=8] {'z_lo','x'}, dimensions={0} | all-to-all | bytes 294912 | tf_op jit(solution)/shard_map/all_to_all | solution.py:211
  135.7 32.8 %all_to_all.27 = f32[32,12,128]{2,1,0:T(8,128)S(1)} all-to-all(f32[32,12,128]{2,1,0:T(8,128)S(1)} %broadcast_in_dim.5), channel_id=1, replica_groups=mesh['z_lo'=6,'x'=4,'z_hi'=2,'core'=2,'rep'=8] {'z_hi','core','rep'}, dimensions={0} | all-to-all | bytes 393216 | tf_op jit(solution)/shard_map/all_to_all | solution.py:195
  168.4 0.6 reduce_sum.19
  (2 shorter events, 0.1 us)
Async XLA Ops:
  1.3 25.5 %all-to-all-start = ((bf16[24,12,128]{2,1,0:T(8,128)(2,1)}), bf16[24,12,128]{2,1,0:T(8,128)(2,1)S(1)}, u32[]{:S(2)}, u32[]{:S(2)}) async-start(bf16[24,12,128]{2,1,0:T(8,128)(2,1)} %broadcast_in_dim.4), calls=%async_computation | async-start | bytes 196608 | tf_op jit(solution)/shard_map/all_to_all | solution.py:195
  26.9 1.9 %copy-start = (bf16[1,1,8,1600,128]{4,3,2,1,0:T(8,128)(2,1)S(1)}, bf16[1,1,8,1600,128]{4,3,2,1,0:T(8,128)(2,1)}, u32[]{:S(2)}) copy-start(bf16[1,1,8,1600,128]{4,3,2,1,0:T(8,128)(2,1)} %param.6) | copy-start | bytes 9830404
  28.8 0.7 copy-start.2
  29.5 0.7 copy-start.4
  30.1 14.6 %copy-start.6 = (bf16[2,1280,320]{1,2,0:T(8,128)(2,1)S(1)}, bf16[2,1280,320]{1,2,0:T(8,128)(2,1)}, u32[]{:S(2)}) copy-start(bf16[2,1280,320]{1,2,0:T(8,128)(2,1)} %param.10) | copy-start | bytes 4915204
  34.4 39.0 %all-to-all-start.1 = ((bf16[48,8,896]{2,1,0:T(8,128)(2,1)}), bf16[48,8,896]{2,1,0:T(8,128)(2,1)S(1)}, u32[]{:S(2)}, u32[]{:S(2)}) async-start(bf16[48,8,896]{2,1,0:T(8,128)(2,1)} %bitcast.4), calls=%async_computation.1 | async-start | bytes 1376256 | tf_op jit(solution)/shard_map/all_to_all | solution.py:206
  44.8 7.5 %collective-permute-start = (bf16[2,1280,320]{1,2,0:T(8,128)(2,1)S(1)}, bf16[2,1280,320]{1,2,0:T(8,128)(2,1)}, u32[]{:S(2)}, u32[]{:S(2)}) collective-permute-start(bf16[2,1280,320]{1,2,0:T(8,128)(2,1)S(1)} %copy-done.6), channel_id=1, source_target_pairs={{0,8},{8,0},{1,9},{9,1},{2,10},{10,2},{3,11},{11,3},{4,12},{12,4},... | collective-permute-start | bytes 4915208 | tf_op jit(solution)/shard_map/ppermute | solution.py:202
  55.9 62.7 %copy-start.3 = (s32[1,1,8]{2,1,0:T(1,128)S(1)}, s32[1,1,8]{2,1,0:T(1,128)}, u32[]{:S(2)}) copy-start(s32[1,1,8]{2,1,0:T(1,128)} %param.8) | copy-start | bytes 100
  73.4 0.8 copy-start.5
  74.3 44.4 %copy-start.1 = (bf16[1,1,8,1600,128]{4,3,2,1,0:T(8,128)(2,1)S(1)}, bf16[1,1,8,1600,128]{4,3,2,1,0:T(8,128)(2,1)}, u32[]{:S(2)}) copy-start(bf16[1,1,8,1600,128]{4,3,2,1,0:T(8,128)(2,1)} %param.6) | copy-start | bytes 9830404

commit v2 on v1

v2 whole, which is shorter than its diff:
```python
import jax
import jax.numpy as jnp
from jax import lax
from jax.experimental import pallas as pl
from jax.experimental.pallas import tpu as pltpu
from jax.sharding import Mesh
from jax.sharding import PartitionSpec as P

BO = 40
NPROBE = 12
HALVES = 2
SIG = BO // HALVES
LANE = 128
F32 = jnp.float32
BF16 = jnp.bfloat16

Z_HI = 2
AUX = ("z_lo", "x")
OUTER = ("z_hi", "z_lo", "x")
LAST = ("core", "rep")


def iota(shape, dim):
    return lax.broadcasted_iota(jnp.int32, shape, dim)


def dot(a, b, ca, cb):
    return lax.dot_general(a, b, (((ca,), (cb,)), ((), ())), preferred_element_type=F32)


def u_kernel(meta_ref, probes_ref, tiles_ref, out_ref, held_ref, sems):
    slot_count, inner, aux_width = tiles_ref.shape
    width = SIG * BO
    copies = [pltpu.make_async_copy(tiles_ref.at[b], held_ref.at[b], sems.at[b]) for b in range(slot_count)]
    for copy in copies:
        copy.start()

    live = meta_ref[2 * slot_count]
    shape = (NPROBE, slot_count, aux_width)
    rows = []
    for b in range(slot_count):
        chosen = probes_ref[meta_ref[b]].astype(F32)
        keep = (iota(shape, 1) == b) & (b < live)
        part = jnp.where(keep, jnp.broadcast_to(chosen[:, None, :], shape), 0.0)
        rows.append(part.reshape(NPROBE * slot_count, aux_width).astype(BF16))
    rows = jnp.concatenate(rows, axis=1)

    tail = out_ref.shape[3] - width
    ids = jnp.zeros((slot_count, tail), F32)
    for b in range(slot_count):
        ids = jnp.where(iota(ids.shape, 0) == b, meta_ref[slot_count + b].astype(F32), ids)
    ids = jnp.broadcast_to(ids[None], (HALVES * NPROBE, slot_count, tail)).astype(BF16)
    for z in range(Z_HI):
        out_ref[z, :, :, width:] = ids

    for copy in copies:
        copy.wait()
    for h in range(HALVES):
        block = jnp.concatenate([held_ref[b, h * width : (h + 1) * width, :] for b in range(slot_count)], axis=1)
        piece = dot(rows, block, 1, 1).reshape(NPROBE, slot_count, width).astype(BF16)
        for z in range(Z_HI):
            out_ref[z, h * NPROBE : (h + 1) * NPROBE, :, :width] = piece


def make_u(tiles, probes_all, meta):
    slot_count = tiles.shape[0]
    chunks = NPROBE * HALVES
    wide = -(-(SIG * BO + 1) // LANE) * LANE
    return pl.pallas_call(
        u_kernel,
        in_specs=[
            pl.BlockSpec(memory_space=pltpu.SMEM),
            pl.BlockSpec(memory_space=pltpu.VMEM),
            pl.BlockSpec(memory_space=pltpu.HBM),
        ],
        out_specs=pl.BlockSpec(memory_space=pltpu.VMEM),
        out_shape=jax.ShapeDtypeStruct((Z_HI, chunks, slot_count, wide), BF16),
        scratch_shapes=[pltpu.VMEM(tiles.shape, BF16), pltpu.SemaphoreType.DMA((slot_count,))],
        compiler_params=pltpu.CompilerParams(vmem_limit_bytes=32 * 2**20),
        name="u_blocks",
    )(meta, probes_all, tiles)


def w_kernel(recv_ref, mine_ref, other_ref, out_ref):
    senders, slot_count, _ = recv_ref.shape
    half = senders // Z_HI
    queue = half * slot_count
    orb = mine_ref.shape[2]
    atoms = orb // BO
    width = SIG * BO

    copies = (iota((BO, orb), 1) % BO == iota((BO, orb), 0)).astype(BF16)
    own_atom = iota((atoms, orb), 1) // BO == iota((atoms, orb), 0)

    hots, spreads = [], []
    for z in range(Z_HI):
        got = recv_ref[z * half : (z + 1) * half].astype(F32).reshape(queue, recv_ref.shape[2])
        ids = got[:, width : width + 1].astype(jnp.int32)
        hot = (iota((queue, atoms), 1) == ids).astype(BF16)
        hots.append(hot)
        spread = dot(hot, got[:, :width].astype(BF16), 0, 0)
        spreads += [spread[:, s * BO : (s + 1) * BO] for s in range(SIG)]
    stacked = jnp.concatenate(spreads, axis=0)
    high = stacked.astype(BF16)
    low = (stacked - high.astype(F32)).astype(BF16)
    count = Z_HI * SIG

    def by_row(part):
        full = dot(part, copies, 1, 0).reshape(count, atoms, orb)
        return jnp.sum(jnp.where(own_atom[None], full, 0.0), axis=1).astype(BF16)

    rows = jnp.concatenate([by_row(high), by_row(low)], axis=0)
    v = None
    for panel in (mine_ref, other_ref):
        w = dot(rows, panel[1], 1, 1)
        w = w[:count] + w[count:]
        part = dot(w.astype(BF16), panel[0], 1, 0)
        v = part if v is None else v + part
    spread_v = jnp.where(own_atom[None], v[:, None, :], 0.0).reshape(count * atoms, orb).astype(BF16)
    spread_v = dot(spread_v, copies, 1, 1)
    for z in range(Z_HI):
        first = z * SIG * atoms
        pieces = [spread_v[first + s * atoms : first + (s + 1) * atoms] for s in range(SIG)]
        table = jnp.concatenate(pieces, axis=1).astype(BF16)
        back = dot(hots[z], table, 1, 0).reshape(half, slot_count, width)
        out_ref[z * half : (z + 1) * half] = back.astype(BF16)


def make_v(recv, mine, other):
    senders, slot_count, _ = recv.shape
    vmem = pl.BlockSpec(memory_space=pltpu.VMEM)
    return pl.pallas_call(
        w_kernel,
        in_specs=[vmem, vmem, vmem],
        out_specs=vmem,
        out_shape=jax.ShapeDtypeStruct((senders, slot_count, SIG * BO), BF16),
        compiler_params=pltpu.CompilerParams(vmem_limit_bytes=40 * 2**20),
        name="w_and_v",
    )(recv, mine, other)


def y_kernel(meta_ref, v_ref, tiles_ref, out_ref, sum_ref):
    slot_count = v_ref.shape[2]
    width = v_ref.shape[3]
    rows = NPROBE * slot_count
    live = meta_ref[2 * slot_count]

    sum_ref[...] = jnp.zeros_like(sum_ref)
    y = None
    for h in range(HALVES):
        block = pl.ds(h * NPROBE, NPROBE)
        total = v_ref[0, block].astype(F32)
        for z in range(1, Z_HI):
            total = total + v_ref[z, block].astype(F32)
        side = jnp.concatenate([tiles_ref[b, h * width : (h + 1) * width, :] for b in range(slot_count)], axis=1)
        part = dot(total.reshape(rows, width).astype(BF16), side, 1, 0)
        y = part if y is None else y + part
    aux_width = tiles_ref.shape[2]
    for b in range(slot_count):
        own = y[:, b * aux_width : (b + 1) * aux_width].reshape(NPROBE, slot_count, aux_width)
        keep = (iota(own.shape, 1) == b) & (b < live)
        sum_ref[meta_ref[b]] += jnp.sum(jnp.where(keep, own, 0.0), axis=1)
    for z in range(Z_HI):
        out_ref[z] = sum_ref[...].astype(BF16)


def make_y(v, tiles, meta, groups):
    aux_width = tiles.shape[2]
    vmem = pl.BlockSpec(memory_space=pltpu.VMEM)
    return pl.pallas_call(
        y_kernel,
        in_specs=[pl.BlockSpec(memory_space=pltpu.SMEM), vmem, vmem],
        out_specs=vmem,
        out_shape=jax.ShapeDtypeStruct((Z_HI, groups, NPROBE, aux_width), BF16),
        scratch_shapes=[pltpu.VMEM((groups, NPROBE, aux_width), F32)],
        compiler_params=pltpu.CompilerParams(vmem_limit_bytes=32 * 2**20),
        name="y_by_owner",
    )(meta, v, tiles)


def everywhere(value, axes):
    count = lax.axis_size(axes)
    copies = jnp.broadcast_to(value[None], (count,) + value.shape)
    return lax.all_to_all(copies, axes, 0, 0)


def body(tiles, atom_of, owner_of, live_count, green, probes):
    tiles = tiles[0, 0]
    slot_count = tiles.shape[0]
    groups = lax.axis_size(AUX)
    meta = jnp.concatenate([owner_of[0, 0], atom_of[0, 0], live_count[0]])
    mine = jnp.swapaxes(green, 1, 2)
    other = lax.ppermute(mine, "core", [(0, 1), (1, 0)])
    probes_all = everywhere(probes, AUX)
    u = make_u(tiles, probes_all, meta)
    u = u.reshape((Z_HI * groups,) + u.shape[2:])
    recv = lax.all_to_all(u, OUTER, 0, 0)
    v = make_v(recv, mine, other)
    v = lax.all_to_all(v, OUTER, 0, 0)
    v = v.reshape(Z_HI, groups, slot_count, SIG * BO)
    y = make_y(v, tiles, meta, groups)
    y = lax.all_to_all(y.reshape((Z_HI * groups,) + y.shape[2:]), OUTER, 0, 0)
    y = jnp.sum(y.astype(F32), axis=0)
    return jnp.sum(everywhere(y, LAST), axis=0)


def solution(mesh):
    aux, orb, rep = mesh.devices.shape
    x = 4
    fine = Mesh(mesh.devices.reshape(aux // x, x, Z_HI, orb // Z_HI, rep), ("z_lo", "x", "z_hi", "core", "rep"))
    orbs = ("z_hi", "core")
    return jax.shard_map(
        body,
        mesh=fine,
        in_specs=(
            P(AUX, orbs + ("rep",), None, None, None),
            P(AUX, orbs + ("rep",), None),
            P(AUX, orbs + ("rep",), None),
            P(AUX, orbs + ("rep",)),
            P(None, None, orbs),
            P(None, AUX),
        ),
        out_specs=P(None, AUX),
        check_vma=False,
    )
```

time: 172 us -> 154 us (0.90); the launches traced: 169 us -> 153 us
  blocking collectives: 82.4 us -> 71.5 us
  local copies, waits for them, and re-layouts: 11.5 us -> 5.89 us
  Pallas kernels: 16 us -> 11.6 us
  waiting for transfers between devices: 27.9 us -> 32 us
    all_to_all x1, blocking collectives: 32.8 us -> 19 us  [everywhere(): return lax.all_to_all(copies, axes, 0, 0)]
    pallas_call x3, Pallas kernels: 16 us -> 11.6 us  [the longest x1 5.91 us: make_v(): pl.pallas_call(w_kernel, in_specs=[vmem, vmem, vmem], out_specs=vmem, out...]
    ppermute x1 -> x0, local copies, waits for them, and re-layouts: 3.68 us -> none  [body(): other = lax.ppermute(green, 'core', [(0, 1), (1, 0)])]
    all_to_all x1, blocking collectives: 14.9 us -> 17.9 us  [body(): y = lax.all_to_all(y.reshape((Z_HI * groups,) + y.shape[2:]), OUTER, 0, 0)]
    all_to_all x1, waiting for transfers between devices: 17.5 us -> 20.1 us  [body(): recv = lax.all_to_all(u, OUTER, 0, 0)]
    ppermute x1, waiting for transfers between devices: 0.84 us -> 3.11 us  [body(): other = lax.ppermute(mine, 'core', [(0, 1), (1, 0)])]
    unnamed x15 -> x10, local copies, waits for them, and re-layouts: 6.49 us -> 4.54 us
  transfers between devices with their start and end apart: 3 -> 3, of which waited for: 3 -> 3; matrix products, arithmetic and copies ran while one was open for 4% -> 0% of each run, Pallas kernels for 0% -> 0%
where the time goes in v2:
time: 154 us; the launch traced here: 153 us
  blocking collectives  71.5 us (46%)
  waiting for transfers between devices  32 us (21%)
  starting transfers between devices  29.9 us (19%)
  Pallas kernels  11.6 us (8%)
  local copies, waits for them, and re-layouts  5.89 us (4%)
    all_to_all x1, blocking collectives, body(): v = lax.all_to_all(v, OUTER, 0, 0)  34.6 us
    all_to_all x1, waiting for transfers between devices, body(): recv = lax.all_to_all(u, OUTER, 0, 0)  20.1 us
    all_to_all x1, blocking collectives, everywhere(): return lax.all_to_all(copies, axes, 0, 0)  19 us
    all_to_all x1, blocking collectives, body(): y = lax.all_to_all(y.reshape((Z_HI * groups,) + y.shape[2:]), OUTER, 0, 0)  17.9 us
    all_to_all x1, starting transfers between devices, everywhere(): return lax.all_to_all(copies, axes, 0, 0)  15.4 us
    all_to_all x1, starting transfers between devices, body(): recv = lax.all_to_all(u, OUTER, 0, 0)  10.3 us
    all_to_all x1, waiting for transfers between devices, everywhere(): return lax.all_to_all(copies, axes, 0, 0)  8.79 us
    pallas_call x1, Pallas kernels, make_v(): pl.pallas_call(w_kernel, in_specs=[vmem, vmem, vmem], out_specs=vmem, out...  5.91 us
  transfers between devices with their start and end apart: 3, of which 3 were waited for; matrix products, arithmetic and copies ran while one was open for 0% of the time, Pallas kernels for 0%

profile of v2, /device:TPU:1, one launch (start us, length us, event | category | flops | bytes accessed | tf_op | source)
XLA Modules:
  0.0 153.0 jit_solution(9304894563663561996)
XLA Ops:
  0.0 1.3 broadcast_in_dim.4
  1.3 15.4 %all-to-all-start = ((bf16[24,12,128]{2,1,0:T(8,128)(2,1)}), bf16[24,12,128]{2,1,0:T(8,128)(2,1)S(1)}, u32[]{:S(2)}, u32[]{:S(2)}) async-start(bf16[24,12,128]{2,1,0:T(8,128)(2,1)} %broadcast_in_dim.4), calls=%async_computation | async-start | bytes 196608 | tf_op jit(solution)/shard_map/all_to_all | solution.py:184
  17.3 0.7 pad_add_fusion.meta_ref
  18.1 8.8 %all-to-all-done.probes_ref = bf16[24,12,128]{2,1,0:T(8,128)(2,1)S(1)} async-done(((bf16[24,12,128]{2,1,0:T(8,128)(2,1)}), bf16[24,12,128]{2,1,0:T(8,128)(2,1)S(1)}, u32[]{:S(2)}, u32[]{:S(2)}) %all-to-all-start) | async-done | bytes 73760 | tf_op jit(solution)/shard_map/all_to_all | solution.py:184
  26.9 0.0 copy-start
  26.9 1.9 %copy-done = bf16[1,1,8,1600,128]{4,3,2,1,0:T(8,128)(2,1)S(1)} copy-done((bf16[1,1,8,1600,128]{4,3,2,1,0:T(8,128)(2,1)S(1)}, bf16[1,1,8,1600,128]{4,3,2,1,0:T(8,128)(2,1)}, u32[]{:S(2)}) %copy-start) | copy-done | bytes 3276824
  28.8 0.0 copy-start.2
  28.8 4.3 %u_blocks.1 = bf16[2,24,8,896]{3,2,1,0:T(8,128)(2,1)} custom-call(s32[17]{0:T(128)S(1)} %pad_add_fusion.meta_ref, bf16[24,12,128]{2,1,0:T(8,128)(2,1)S(1)} %all-to-all-done.probes_ref, bf16[8,1600,128]{2,1,0:T(8,128)(2,1)S(1)} %bitcast.9), custom_call_target="tpu_custom_call" | custom-call | tf_op jit(solution)/shard_map/u_blocks/pallas_call | solution.py:69
  33.1 10.3 %all-to-all-start.1 = ((bf16[48,8,896]{2,1,0:T(8,128)(2,1)}), bf16[48,8,896]{2,1,0:T(8,128)(2,1)S(1)}, u32[]{:S(2)}, u32[]{:S(2)}) async-start(bf16[48,8,896]{2,1,0:T(8,128)(2,1)} %bitcast.4), calls=%async_computation.1 | async-start | bytes 1376256 | tf_op jit(solution)/shard_map/all_to_all | solution.py:197
  43.5 0.0 copy-done.2
  43.5 4.3 %collective-permute-start = (bf16[2,320,1280]{2,1,0:T(8,128)(2,1)S(1)}, bf16[2,320,1280]{2,1,0:T(8,128)(2,1)S(1)}, u32[]{:S(2)}, u32[]{:S(2)}) collective-permute-start(bf16[2,320,1280]{2,1,0:T(8,128)(2,1)S(1)} %bitcast.12), channel_id=1, source_target_pairs={{0,8},{8,0},{1,9},{9,1},{2,10},{10,2},{3,11},{11,3},{4,12},{12,4},... | collective-permute-start | bytes 4915208 | tf_op jit(solution)/shard_map/ppermute | solution.py:193
  47.7 3.1 %collective-permute-done.other_ref = bf16[2,320,1280]{2,1,0:T(8,128)(2,1)S(1)} collective-permute-done((bf16[2,320,1280]{2,1,0:T(8,128)(2,1)S(1)}, bf16[2,320,1280]{2,1,0:T(8,128)(2,1)S(1)}, u32[]{:S(2)}, u32[]{:S(2)}) %collective-permute-start) | collective-permute-done | bytes 1638432 | tf_op jit(solution)/shard_map/ppermute | solution.py:193
  50.9 0.0 copy-start.3
  50.9 1.2 copy-done.3
  52.0 20.1 %all-to-all-done.1.recv_ref = bf16[48,8,896]{2,1,0:T(8,128)(2,1)S(1)} async-done(((bf16[48,8,896]{2,1,0:T(8,128)(2,1)}), bf16[48,8,896]{2,1,0:T(8,128)(2,1)S(1)}, u32[]{:S(2)}, u32[]{:S(2)}) %all-to-all-start.1) | async-done | bytes 688160 | tf_op jit(solution)/shard_map/all_to_all | solution.py:197
  72.2 0.0 copy-start.4
  72.2 1.4 copy-done.4
  73.6 0.0 copy-start.1
  73.6 5.9 %w_and_v.1 = bf16[48,8,800]{2,1,0:T(8,128)(2,1)S(1)} custom-call(bf16[48,8,896]{2,1,0:T(8,128)(2,1)S(1)} %all-to-all-done.1.recv_ref, bf16[2,320,1280]{2,1,0:T(8,128)(2,1)S(1)} %bitcast.13, bf16[2,320,1280]{2,1,0:T(8,128)(2,1)S(1)} %copy-done.4), custom_call_target="tpu_custom_call" | custom-call | tf_op jit(solution)/shard_map/w_and_v/pallas_call | solution.py:132
  79.5 34.6 %all_to_all.25 = bf16[48,8,800]{2,1,0:T(8,128)(2,1)S(1)} all-to-all(bf16[48,8,800]{2,1,0:T(8,128)(2,1)S(1)} %w_and_v.1), channel_id=1, replica_groups=mesh['z_lo'=6,'x'=4,'z_hi'=2,'core'=2,'rep'=8] {'z_hi','z_lo','x'}, dimensions={0} | all-to-all | bytes 1228800 | tf_op jit(solution)/shard_map/all_to_all | solution.py:199
  114.1 0.0 copy-done.1
  114.1 1.4 y_by_owner.1
  115.5 17.9 %all_to_all.26 = bf16[48,12,128]{2,1,0:T(8,128)(2,1)S(1)} all-to-all(bf16[48,12,128]{2,1,0:T(8,128)(2,1)S(1)} %bitcast.14), channel_id=1, replica_groups=mesh['z_lo'=6,'x'=4,'z_hi'=2,'core'=2,'rep'=8] {'z_hi','z_lo','x'}, dimensions={0} | all-to-all | bytes 294912 | tf_op jit(solution)/shard_map/all_to_all | solution.py:202
  133.4 0.1 convert_reduce_fusion
  133.4 19.0 %all_to_all.27 = f32[16,12,128]{2,1,0:T(8,128)S(1)} all-to-all(f32[16,12,128]{2,1,0:T(8,128)S(1)} %broadcast_in_dim.5), channel_id=1, replica_groups=mesh['z_lo'=6,'x'=4,'z_hi'=2,'core'=2,'rep'=8] {'core','rep'}, dimensions={0} | all-to-all | bytes 196608 | tf_op jit(solution)/shard_map/all_to_all | solution.py:184
  152.4 0.6 reduce_sum.19
  (1 shorter events, 0.0 us)
Async XLA Ops:
  1.3 25.5 %all-to-all-start = ((bf16[24,12,128]{2,1,0:T(8,128)(2,1)}), bf16[24,12,128]{2,1,0:T(8,128)(2,1)S(1)}, u32[]{:S(2)}, u32[]{:S(2)}) async-start(bf16[24,12,128]{2,1,0:T(8,128)(2,1)} %broadcast_in_dim.4), calls=%async_computation | async-start | bytes 196608 | tf_op jit(solution)/shard_map/all_to_all | solution.py:184
  26.9 1.9 %copy-start = (bf16[1,1,8,1600,128]{4,3,2,1,0:T(8,128)(2,1)S(1)}, bf16[1,1,8,1600,128]{4,3,2,1,0:T(8,128)(2,1)}, u32[]{:S(2)}) copy-start(bf16[1,1,8,1600,128]{4,3,2,1,0:T(8,128)(2,1)} %param.6) | copy-start | bytes 9830404
  28.8 14.7 %copy-start.2 = (bf16[2,1280,320]{1,2,0:T(8,128)(2,1)S(1)}, bf16[2,1280,320]{1,2,0:T(8,128)(2,1)}, u32[]{:S(2)}) copy-start(bf16[2,1280,320]{1,2,0:T(8,128)(2,1)} %param.10) | copy-start | bytes 4915204
  33.1 39.0 %all-to-all-start.1 = ((bf16[48,8,896]{2,1,0:T(8,128)(2,1)}), bf16[48,8,896]{2,1,0:T(8,128)(2,1)S(1)}, u32[]{:S(2)}, u32[]{:S(2)}) async-start(bf16[48,8,896]{2,1,0:T(8,128)(2,1)} %bitcast.4), calls=%async_computation.1 | async-start | bytes 1376256 | tf_op jit(solution)/shard_map/all_to_all | solution.py:197
  43.5 7.4 %collective-permute-start = (bf16[2,320,1280]{2,1,0:T(8,128)(2,1)S(1)}, bf16[2,320,1280]{2,1,0:T(8,128)(2,1)S(1)}, u32[]{:S(2)}, u32[]{:S(2)}) collective-permute-start(bf16[2,320,1280]{2,1,0:T(8,128)(2,1)S(1)} %bitcast.12), channel_id=1, source_target_pairs={{0,8},{8,0},{1,9},{9,1},{2,10},{10,2},{3,11},{11,3},{4,12},{12,4},... | collective-permute-start | bytes 4915208 | tf_op jit(solution)/shard_map/ppermute | solution.py:193
  50.9 1.2 copy-start.3
  72.2 1.4 copy-start.4
  73.6 40.5 %copy-start.1 = (bf16[1,1,8,1600,128]{4,3,2,1,0:T(8,128)(2,1)S(1)}, bf16[1,1,8,1600,128]{4,3,2,1,0:T(8,128)(2,1)}, u32[]{:S(2)}) copy-start(bf16[1,1,8,1600,128]{4,3,2,1,0:T(8,128)(2,1)} %param.6) | copy-start | bytes 9830404

commit v3 on v2

--- a/solution.py
+++ b/solution.py
@@ -28,13 +28,36 @@
     return lax.dot_general(a, b, (((ca,), (cb,)), ((), ())), preferred_element_type=F32)
 
 
-def u_kernel(meta_ref, probes_ref, tiles_ref, out_ref, held_ref, sems):
-    slot_count, inner, aux_width = tiles_ref.shape
+def turn_kernel(tiles_ref, out_ref, held_ref, sems):
+    slot_count, _, aux_width = tiles_ref.shape
     width = SIG * BO
     copies = [pltpu.make_async_copy(tiles_ref.at[b], held_ref.at[b], sems.at[b]) for b in range(slot_count)]
     for copy in copies:
         copy.start()
-
+    for b, copy in enumerate(copies):
+        copy.wait()
+        for h in range(HALVES):
+            out_ref[h, b * aux_width : (b + 1) * aux_width, :] = held_ref[b, h * width : (h + 1) * width, :].T
+
+
+def turn(tiles):
+    slot_count, inner, aux_width = tiles.shape
+    return pl.pallas_call(
+        turn_kernel,
+        in_specs=[pl.BlockSpec(memory_space=pltpu.HBM)],
+        out_specs=pl.BlockSpec(memory_space=pltpu.VMEM),
+        out_shape=jax.ShapeDtypeStruct((HALVES, slot_count * aux_width, inner // HALVES), BF16),
+        scratch_shapes=[pltpu.VMEM(tiles.shape, BF16), pltpu.SemaphoreType.DMA((slot_count,))],
+        compiler_params=pltpu.CompilerParams(vmem_limit_bytes=24 * 2**20),
+        cost_estimate=pl.CostEstimate(flops=0, bytes_accessed=4 * tiles.size, transcendentals=0),
+        name="turn_tiles",
+    )(tiles)
+
+
+def u_kernel(meta_ref, probes_ref, turned_ref, out_ref):
+    slot_count = out_ref.shape[2]
+    aux_width = probes_ref.shape[2]
+    width = SIG * BO
     live = meta_ref[2 * slot_count]
     shape = (NPROBE, slot_count, aux_width)
     rows = []
@@ -53,32 +76,24 @@
     for z in range(Z_HI):
         out_ref[z, :, :, width:] = ids
 
-    for copy in copies:
-        copy.wait()
     for h in range(HALVES):
-        block = jnp.concatenate([held_ref[b, h * width : (h + 1) * width, :] for b in range(slot_count)], axis=1)
-        piece = dot(rows, block, 1, 1).reshape(NPROBE, slot_count, width).astype(BF16)
+        piece = dot(rows, turned_ref[h], 1, 0).reshape(NPROBE, slot_count, width).astype(BF16)
         for z in range(Z_HI):
             out_ref[z, h * NPROBE : (h + 1) * NPROBE, :, :width] = piece
 
 
-def make_u(tiles, probes_all, meta):
-    slot_count = tiles.shape[0]
+def make_u(turned, probes_all, meta, slot_count):
     chunks = NPROBE * HALVES
     wide = -(-(SIG * BO + 1) // LANE) * LANE
+    vmem = pl.BlockSpec(memory_space=pltpu.VMEM)
     return pl.pallas_call(
         u_kernel,
-        in_specs=[
-            pl.BlockSpec(memory_space=pltpu.SMEM),
-            pl.BlockSpec(memory_space=pltpu.VMEM),
-            pl.BlockSpec(memory_space=pltpu.HBM),
-        ],
-        out_specs=pl.BlockSpec(memory_space=pltpu.VMEM),
+        in_specs=[pl.BlockSpec(memory_space=pltpu.SMEM), vmem, vmem],
+        out_specs=vmem,
         out_shape=jax.ShapeDtypeStruct((Z_HI, chunks, slot_count, wide), BF16),
-        scratch_shapes=[pltpu.VMEM(tiles.shape, BF16), pltpu.SemaphoreType.DMA((slot_count,))],
         compiler_params=pltpu.CompilerParams(vmem_limit_bytes=32 * 2**20),
         name="u_blocks",
-    )(meta, probes_all, tiles)
+    )(meta, probes_all, turned)
 
 
 def w_kernel(recv_ref, mine_ref, other_ref, out_ref):
@@ -192,7 +207,8 @@
     mine = jnp.swapaxes(green, 1, 2)
     other = lax.ppermute(mine, "core", [(0, 1), (1, 0)])
     probes_all = everywhere(probes, AUX)
-    u = make_u(tiles, probes_all, meta)
+    probes_all, other = lax.optimization_barrier((probes_all, other))
+    u = make_u(turn(tiles), probes_all, meta, slot_count)
     u = u.reshape((Z_HI * groups,) + u.shape[2:])
     recv = lax.all_to_all(u, OUTER, 0, 0)
     v = make_v(recv, mine, other)

time: 154 us -> 151 us (0.981)
  blocking collectives: 71.5 us -> 110 us
  waiting for transfers between devices: 32 us -> 3 us
  starting transfers between devices: 29.9 us -> 17.9 us
    all_to_all x0 -> x1, blocking collectives: none -> 38.5 us  [body(): recv = lax.all_to_all(u, OUTER, 0, 0)]
    all_to_all x1 -> x0, waiting for transfers between devices: 20.1 us -> none  [body(): recv = lax.all_to_all(u, OUTER, 0, 0)]
    all_to_all x1 -> x0, starting transfers between devices: 10.3 us -> none  [body(): recv = lax.all_to_all(u, OUTER, 0, 0)]
    all_to_all x1, starting transfers between devices: 15.4 us -> 5.51 us  [everywhere(): return lax.all_to_all(copies, axes, 0, 0)]
    ppermute x1, starting transfers between devices: 4.25 us -> 12.4 us  [body(): other = lax.ppermute(mine, 'core', [(0, 1), (1, 0)])]
    all_to_all x1, waiting for transfers between devices: 8.79 us -> 3 us  [everywhere(): return lax.all_to_all(copies, axes, 0, 0)]
    pallas_call x0 -> x1, Pallas kernels: none -> 3.13 us  [turn(): pl.pallas_call(turn_kernel, in_specs=[pl.BlockSpec(memory_space=pltpu.HBM...]
    ppermute x1, waiting for transfers between devices: 3.11 us -> 0.01 us  [body(): other = lax.ppermute(mine, 'core', [(0, 1), (1, 0)])]
  transfers between devices with their start and end apart: 3 -> 2, of which waited for: 3 -> 1; matrix products, arithmetic and copies ran while one was open for 0% -> 1% of each run, Pallas kernels for 0% -> 2%
where the time goes in v3:
time: 151 us
  blocking collectives  110 us (73%)
  starting transfers between devices  17.9 us (12%)
  Pallas kernels  11.7 us (8%)
  local copies, waits for them, and re-layouts  7.11 us (5%)
  waiting for transfers between devices  3 us (2%)
    all_to_all x1, blocking collectives, body(): recv = lax.all_to_all(u, OUTER, 0, 0)  38.5 us
    all_to_all x1, blocking collectives, body(): v = lax.all_to_all(v, OUTER, 0, 0)  34.7 us
    all_to_all x1, blocking collectives, everywhere(): return lax.all_to_all(copies, axes, 0, 0)  19 us
    all_to_all x1, blocking collectives, body(): y = lax.all_to_all(y.reshape((Z_HI * groups,) + y.shape[2:]), OUTER, 0, 0)  17.8 us
    ppermute x1, starting transfers between devices, body(): other = lax.ppermute(mine, 'core', [(0, 1), (1, 0)])  12.4 us
    pallas_call x1, Pallas kernels, make_v(): pl.pallas_call(w_kernel, in_specs=[vmem, vmem, vmem], out_specs=vmem, out...  5.9 us
    unnamed x14, local copies, waits for them, and re-layouts  5.76 us
    all_to_all x1, starting transfers between devices, everywhere(): return lax.all_to_all(copies, axes, 0, 0)  5.51 us
  transfers between devices with their start and end apart: 2, of which 1 were waited for; matrix products, arithmetic and copies ran while one was open for 1% of the time, Pallas kernels for 2%

profile of v3, /device:TPU:1, one launch (start us, length us, event | category | flops | bytes accessed | tf_op | source)
XLA Modules:
  0.0 151.0 jit_solution(14521762717150896256)
XLA Ops:
  0.0 12.4 %collective-permute-start = (bf16[2,320,1280]{2,1,0:T(8,128)(2,1)}, bf16[2,320,1280]{2,1,0:T(8,128)(2,1)S(1)}, u32[]{:S(2)}, u32[]{:S(2)}) collective-permute-start(bf16[2,320,1280]{2,1,0:T(8,128)(2,1)} %bitcast.13), channel_id=1, source_target_pairs={{0,8},{8,0},{1,9},{9,1},{2,10},{10,2},{3,11},{11,3},{4,12},{12,4},... | collective-permute-start | bytes 4915208 | tf_op jit(solution)/shard_map/ppermute | solution.py:208
  12.4 1.3 broadcast_in_dim.4
  13.8 5.5 %all-to-all-start = ((bf16[24,12,128]{2,1,0:T(8,128)(2,1)}), bf16[24,12,128]{2,1,0:T(8,128)(2,1)S(1)}, u32[]{:S(2)}, u32[]{:S(2)}) async-start(bf16[24,12,128]{2,1,0:T(8,128)(2,1)} %broadcast_in_dim.4), calls=%async_computation | async-start | bytes 196608 | tf_op jit(solution)/shard_map/all_to_all | solution.py:199
  19.9 0.0 copy-start.2
  19.9 1.9 %copy-done.2 = bf16[1,1,8,1600,128]{4,3,2,1,0:T(8,128)(2,1)S(1)} copy-done((bf16[1,1,8,1600,128]{4,3,2,1,0:T(8,128)(2,1)S(1)}, bf16[1,1,8,1600,128]{4,3,2,1,0:T(8,128)(2,1)}, u32[]{:S(2)}) %copy-start.2) | copy-done | bytes 3276824
  21.9 0.0 copy-start.5
  21.9 0.0 copy-start.6
  21.9 0.0 copy-start.4
  21.9 3.1 %turn_tiles.1.turned_ref = bf16[2,1024,800]{2,1,0:T(8,128)(2,1)S(1)} custom-call(bf16[8,1600,128]{2,1,0:T(8,128)(2,1)S(1)} %bitcast.9), custom_call_target="tpu_custom_call" | custom-call | bytes 6553600 | tf_op jit(solution)/shard_map/turn_tiles/pallas_call | solution.py:45
  25.0 0.0 copy-start
  25.0 1.8 %copy-done = bf16[2,1024,800]{2,1,0:T(8,128)(2,1)} copy-done((bf16[2,1024,800]{2,1,0:T(8,128)(2,1)}, bf16[2,1024,800]{2,1,0:T(8,128)(2,1)S(1)}, u32[]{:S(2)}) %copy-start) | copy-done | bytes 3276824
  26.8 0.0 copy-done.5
  26.8 0.0 copy-done.6
  26.8 0.1 pad_add_fusion.meta_ref
  26.9 3.0 %all-to-all-done.probes_ref = bf16[24,12,128]{2,1,0:T(8,128)(2,1)S(1)} async-done(((bf16[24,12,128]{2,1,0:T(8,128)(2,1)}), bf16[24,12,128]{2,1,0:T(8,128)(2,1)S(1)}, u32[]{:S(2)}, u32[]{:S(2)}) %all-to-all-start) | async-done | bytes 73760 | tf_op jit(solution)/shard_map/all_to_all | solution.py:199
  29.9 0.0 collective-permute-done.other_ref
  29.9 0.0 copy-start.1
  29.9 2.0 %copy-done.1 = bf16[2,1024,800]{2,1,0:T(8,128)(2,1)S(1)} copy-done((bf16[2,1024,800]{2,1,0:T(8,128)(2,1)S(1)}, bf16[2,1024,800]{2,1,0:T(8,128)(2,1)}, u32[]{:S(2)}) %copy-start.1) | copy-done | bytes 3276824
  31.9 1.3 u_blocks.1
  33.2 38.5 %all_to_all.25.recv_ref = bf16[48,8,896]{2,1,0:T(8,128)(2,1)S(1)} all-to-all(bf16[48,8,896]{2,1,0:T(8,128)(2,1)S(1)} %bitcast.11), channel_id=1, replica_groups=mesh['z_lo'=6,'x'=4,'z_hi'=2,'core'=2,'rep'=8] {'z_hi','z_lo','x'}, dimensions={0} | all-to-all | bytes 1376256 | tf_op jit(solution)/shard_map/all_to_all | solution.py:213
  71.7 0.0 copy-done.4
  71.7 0.0 copy-start.3
  71.7 5.9 %w_and_v.1 = bf16[48,8,800]{2,1,0:T(8,128)(2,1)S(1)} custom-call(bf16[48,8,896]{2,1,0:T(8,128)(2,1)S(1)} %all_to_all.25.recv_ref, bf16[2,320,1280]{2,1,0:T(8,128)(2,1)S(1)} %bitcast.14, bf16[2,320,1280]{2,1,0:T(8,128)(2,1)S(1)} %collective-permute-done.other_ref), custom_call_target="tpu_custom_call" | custom-call | tf_op jit(solution)/shard_map/w_and_v/pallas_call | solution.py:147
  77.6 34.7 %all_to_all.26 = bf16[48,8,800]{2,1,0:T(8,128)(2,1)S(1)} all-to-all(bf16[48,8,800]{2,1,0:T(8,128)(2,1)S(1)} %w_and_v.1), channel_id=1, replica_groups=mesh['z_lo'=6,'x'=4,'z_hi'=2,'core'=2,'rep'=8] {'z_hi','z_lo','x'}, dimensions={0} | all-to-all | bytes 1228800 | tf_op jit(solution)/shard_map/all_to_all | solution.py:215
  112.2 0.0 copy-done.3
  112.2 1.4 y_by_owner.1
  113.6 17.8 %all_to_all.27 = bf16[48,12,128]{2,1,0:T(8,128)(2,1)S(1)} all-to-all(bf16[48,12,128]{2,1,0:T(8,128)(2,1)S(1)} %bitcast.15), channel_id=1, replica_groups=mesh['z_lo'=6,'x'=4,'z_hi'=2,'core'=2,'rep'=8] {'z_hi','z_lo','x'}, dimensions={0} | all-to-all | bytes 294912 | tf_op jit(solution)/shard_map/all_to_all | solution.py:218
  131.4 0.1 convert_reduce_fusion
  131.4 19.0 %all_to_all.28 = f32[16,12,128]{2,1,0:T(8,128)S(1)} all-to-all(f32[16,12,128]{2,1,0:T(8,128)S(1)} %broadcast_in_dim.5), channel_id=1, replica_groups=mesh['z_lo'=6,'x'=4,'z_hi'=2,'core'=2,'rep'=8] {'core','rep'}, dimensions={0} | all-to-all | bytes 196608 | tf_op jit(solution)/shard_map/all_to_all | solution.py:199
  150.4 0.6 reduce_sum.19
  (1 shorter events, 0.0 us)
Async XLA Ops:
  0.0 29.9 %collective-permute-start = (bf16[2,320,1280]{2,1,0:T(8,128)(2,1)}, bf16[2,320,1280]{2,1,0:T(8,128)(2,1)S(1)}, u32[]{:S(2)}, u32[]{:S(2)}) collective-permute-start(bf16[2,320,1280]{2,1,0:T(8,128)(2,1)} %bitcast.13), channel_id=1, source_target_pairs={{0,8},{8,0},{1,9},{9,1},{2,10},{10,2},{3,11},{11,3},{4,12},{12,4},... | collective-permute-start | bytes 4915208 | tf_op jit(solution)/shard_map/ppermute | solution.py:208
  13.8 16.1 %all-to-all-start = ((bf16[24,12,128]{2,1,0:T(8,128)(2,1)}), bf16[24,12,128]{2,1,0:T(8,128)(2,1)S(1)}, u32[]{:S(2)}, u32[]{:S(2)}) async-start(bf16[24,12,128]{2,1,0:T(8,128)(2,1)} %broadcast_in_dim.4), calls=%async_computation | async-start | bytes 196608 | tf_op jit(solution)/shard_map/all_to_all | solution.py:199
  19.9 1.9 %copy-start.2 = (bf16[1,1,8,1600,128]{4,3,2,1,0:T(8,128)(2,1)S(1)}, bf16[1,1,8,1600,128]{4,3,2,1,0:T(8,128)(2,1)}, u32[]{:S(2)}) copy-start(bf16[1,1,8,1600,128]{4,3,2,1,0:T(8,128)(2,1)} %param.6) | copy-start | bytes 9830404
  21.9 4.9 %copy-start.5 = (s32[1,1,8]{2,1,0:T(1,128)S(1)}, s32[1,1,8]{2,1,0:T(1,128)}, u32[]{:S(2)}) copy-start(s32[1,1,8]{2,1,0:T(1,128)} %param.7) | copy-start | bytes 100
  21.9 4.9 %copy-start.6 = (s32[1,1,8]{2,1,0:T(1,128)S(1)}, s32[1,1,8]{2,1,0:T(1,128)}, u32[]{:S(2)}) copy-start(s32[1,1,8]{2,1,0:T(1,128)} %param.8) | copy-start | bytes 100
  21.9 49.8 %copy-start.4 = (bf16[2,1280,320]{1,2,0:T(8,128)(2,1)S(1)}, bf16[2,1280,320]{1,2,0:T(8,128)(2,1)}, u32[]{:S(2)}) copy-start(bf16[2,1280,320]{1,2,0:T(8,128)(2,1)} %param.10) | copy-start | bytes 4915204
  25.0 1.8 %copy-start = (bf16[2,1024,800]{2,1,0:T(8,128)(2,1)}, bf16[2,1024,800]{2,1,0:T(8,128)(2,1)S(1)}, u32[]{:S(2)}) copy-start(bf16[2,1024,800]{2,1,0:T(8,128)(2,1)S(1)} %turn_tiles.1.turned_ref) | copy-start | bytes 9830404
  29.9 2.0 %copy-start.1 = (bf16[2,1024,800]{2,1,0:T(8,128)(2,1)S(1)}, bf16[2,1024,800]{2,1,0:T(8,128)(2,1)}, u32[]{:S(2)}) copy-start(bf16[2,1024,800]{2,1,0:T(8,128)(2,1)} %copy-done) | copy-start | bytes 9830404
  71.7 40.6 %copy-start.3 = (bf16[1,1,8,1600,128]{4,3,2,1,0:T(8,128)(2,1)S(1)}, bf16[1,1,8,1600,128]{4,3,2,1,0:T(8,128)(2,1)}, u32[]{:S(2)}) copy-start(bf16[1,1,8,1600,128]{4,3,2,1,0:T(8,128)(2,1)} %param.6) | copy-start | bytes 9830404

commit v4 on v3

v4 whole, which is shorter than its diff:
```python
import jax
import jax.numpy as jnp
from jax import lax
from jax.experimental import pallas as pl
from jax.experimental.pallas import tpu as pltpu
from jax.sharding import Mesh
from jax.sharding import PartitionSpec as P

BO = 40
NPROBE = 12
HALVES = 2
SIG = BO // HALVES
LANE = 128
F32 = jnp.float32
BF16 = jnp.bfloat16

Z_HI = 2
AUX = ("z_lo", "x")
OUTER = ("z_hi", "z_lo", "x")
LAST = ("core", "rep")


def iota(shape, dim):
    return lax.broadcasted_iota(jnp.int32, shape, dim)


def dot(a, b, ca, cb):
    return lax.dot_general(a, b, (((ca,), (cb,)), ((), ())), preferred_element_type=F32)


def turn_kernel(tiles_ref, out_ref, held_ref, sems):
    slot_count, _, aux_width = tiles_ref.shape
    width = SIG * BO
    copies = [pltpu.make_async_copy(tiles_ref.at[b], held_ref.at[b], sems.at[b]) for b in range(slot_count)]
    for copy in copies:
        copy.start()
    for b, copy in enumerate(copies):
        copy.wait()
        for h in range(HALVES):
            out_ref[h, b * aux_width : (b + 1) * aux_width, :] = held_ref[b, h * width : (h + 1) * width, :].T


def turn(tiles):
    slot_count, inner, aux_width = tiles.shape
    return pl.pallas_call(
        turn_kernel,
        in_specs=[pl.BlockSpec(memory_space=pltpu.HBM)],
        out_specs=pl.BlockSpec(memory_space=pltpu.VMEM),
        out_shape=jax.ShapeDtypeStruct((HALVES, slot_count * aux_width, inner // HALVES), BF16),
        scratch_shapes=[pltpu.VMEM(tiles.shape, BF16), pltpu.SemaphoreType.DMA((slot_count,))],
        compiler_params=pltpu.CompilerParams(vmem_limit_bytes=24 * 2**20),
        cost_estimate=pl.CostEstimate(flops=0, bytes_accessed=4 * tiles.size, transcendentals=0),
        name="turn_tiles",
    )(tiles)


def u_kernel(meta_ref, probes_ref, turned_ref, out_ref):
    slot_count = out_ref.shape[1]
    aux_width = probes_ref.shape[2]
    width = SIG * BO
    live = meta_ref[2 * slot_count]
    shape = (NPROBE, slot_count, aux_width)
    rows = []
    for b in range(slot_count):
        chosen = probes_ref[meta_ref[b]].astype(F32)
        keep = (iota(shape, 1) == b) & (b < live)
        part = jnp.where(keep, jnp.broadcast_to(chosen[:, None, :], shape), 0.0)
        rows.append(part.reshape(NPROBE * slot_count, aux_width).astype(BF16))
    rows = jnp.concatenate(rows, axis=1)

    tail = out_ref.shape[2] - width
    ids = jnp.zeros((slot_count, tail), F32)
    for b in range(slot_count):
        ids = jnp.where(iota(ids.shape, 0) == b, meta_ref[slot_count + b].astype(F32), ids)
    ids = jnp.broadcast_to(ids[None], (HALVES * NPROBE, slot_count, tail)).astype(BF16)
    out_ref[:, :, width:] = ids

    for h in range(HALVES):
        piece = dot(rows, turned_ref[h], 1, 0).reshape(NPROBE, slot_count, width).astype(BF16)
        out_ref[h * NPROBE : (h + 1) * NPROBE, :, :width] = piece


def make_u(turned, probes_all, meta, slot_count):
    chunks = NPROBE * HALVES
    wide = -(-(SIG * BO + 1) // LANE) * LANE
    vmem = pl.BlockSpec(memory_space=pltpu.VMEM)
    return pl.pallas_call(
        u_kernel,
        in_specs=[pl.BlockSpec(memory_space=pltpu.SMEM), vmem, vmem],
        out_specs=vmem,
        out_shape=jax.ShapeDtypeStruct((chunks, slot_count, wide), BF16),
        compiler_params=pltpu.CompilerParams(vmem_limit_bytes=32 * 2**20),
        name="u_blocks",
    )(meta, probes_all, turned)


def spreader(orb):
    copies = (iota((BO, orb), 1) % BO == iota((BO, orb), 0)).astype(BF16)
    return copies, iota((orb // BO, orb), 1) // BO == iota((orb // BO, orb), 0)


def atoms_of(recv_ref, atoms):
    senders, slot_count, wide = recv_ref.shape
    ids = recv_ref[:, :, SIG * BO :].astype(F32).reshape(senders * slot_count, wide - SIG * BO)[:, :1].astype(jnp.int32)
    return (iota((senders * slot_count, atoms), 1) == ids).astype(BF16)


def through(rows, panels):
    v = None
    for panel in panels:
        w = dot(rows, panel[1], 1, 1)
        if w.shape[0] > SIG:
            w = w[:SIG] + w[SIG:]
        part = dot(w.astype(BF16), panel[0], 1, 0)
        v = part if v is None else v + part
    return v


def by_atom(recv_ref, orb, rest):
    senders, slot_count, _ = recv_ref.shape
    width = SIG * BO
    atoms = orb // BO
    copies, own_atom = spreader(orb)
    got = recv_ref[:, :, :width].astype(F32).reshape(senders * slot_count, width).astype(BF16)
    spread = dot(atoms_of(recv_ref, atoms), got, 0, 0)
    stacked = jnp.concatenate([spread[:, s * BO : (s + 1) * BO] for s in range(SIG)], axis=0)
    high = stacked.astype(BF16)

    def by_row(part):
        full = dot(part, copies, 1, 0).reshape(SIG, atoms, orb)
        return jnp.sum(jnp.where(own_atom[None], full, 0.0), axis=1).astype(BF16)

    if not rest:
        return by_row(high)
    low = (stacked - high.astype(F32)).astype(BF16)
    return jnp.concatenate([by_row(high), by_row(low)], axis=0)


def sum_kernel(recv_ref, rows_ref):
    rows_ref[...] = by_atom(recv_ref, rows_ref.shape[1], False)


def near_kernel(recv_ref, mine_ref, other_ref, out_ref):
    out_ref[...] = through(by_atom(recv_ref, out_ref.shape[1], True), (mine_ref, other_ref))


def far_kernel(rows_ref, mine_ref, other_ref, out_ref):
    out_ref[...] = through(rows_ref[...], (mine_ref, other_ref)).astype(BF16)


def back_kernel(recv_ref, near_ref, far_ref, out_ref):
    senders, slot_count, _ = recv_ref.shape
    orb = near_ref.shape[1]
    atoms = orb // BO
    copies, own_atom = spreader(orb)
    v = near_ref[...] + far_ref[...].astype(F32)
    table = jnp.where(own_atom[None], v[:, None, :], 0.0).reshape(SIG * atoms, orb).astype(BF16)
    table = dot(table, copies, 1, 1)
    table = jnp.concatenate([table[s * atoms : (s + 1) * atoms] for s in range(SIG)], axis=1).astype(BF16)
    back = dot(atoms_of(recv_ref, atoms), table, 1, 0)
    out_ref[...] = back.reshape(senders, slot_count, SIG * BO).astype(BF16)


def on_vmem(kernel, out_shape, name, *args):
    vmem = pl.BlockSpec(memory_space=pltpu.VMEM)
    return pl.pallas_call(
        kernel,
        in_specs=[vmem] * len(args),
        out_specs=vmem,
        out_shape=out_shape,
        compiler_params=pltpu.CompilerParams(vmem_limit_bytes=24 * 2**20),
        name=name,
    )(*args)


def make_rows(recv, orb):
    return on_vmem(sum_kernel, jax.ShapeDtypeStruct((SIG, orb), BF16), "u_by_atom", recv)


def make_near(recv, mine, other):
    shape = jax.ShapeDtypeStruct((SIG, mine.shape[2]), F32)
    return on_vmem(near_kernel, shape, "v_near", recv, mine, other)


def make_far(rows, mine, other):
    return on_vmem(far_kernel, jax.ShapeDtypeStruct(rows.shape, BF16), "v_far", rows, mine, other)


def make_back(recv, near, far):
    shape = jax.ShapeDtypeStruct(recv.shape[:2] + (SIG * BO,), BF16)
    return on_vmem(back_kernel, shape, "v_back", recv, near, far)


def y_kernel(meta_ref, v_ref, tiles_ref, out_ref, sum_ref):
    slot_count = v_ref.shape[1]
    width = v_ref.shape[2]
    rows = NPROBE * slot_count
    live = meta_ref[2 * slot_count]

    sum_ref[...] = jnp.zeros_like(sum_ref)
    y = None
    for h in range(HALVES):
        total = v_ref[h * NPROBE : (h + 1) * NPROBE].astype(F32)
        side = jnp.concatenate([tiles_ref[b, h * width : (h + 1) * width, :] for b in range(slot_count)], axis=1)
        part = dot(total.reshape(rows, width).astype(BF16), side, 1, 0)
        y = part if y is None else y + part
    aux_width = tiles_ref.shape[2]
    for b in range(slot_count):
        own = y[:, b * aux_width : (b + 1) * aux_width].reshape(NPROBE, slot_count, aux_width)
        keep = (iota(own.shape, 1) == b) & (b < live)
        sum_ref[meta_ref[b]] += jnp.sum(jnp.where(keep, own, 0.0), axis=1)
    for z in range(Z_HI):
        out_ref[z] = sum_ref[...].astype(BF16)


def make_y(v, tiles, meta, groups):
    aux_width = tiles.shape[2]
    vmem = pl.BlockSpec(memory_space=pltpu.VMEM)
    return pl.pallas_call(
        y_kernel,
        in_specs=[pl.BlockSpec(memory_space=pltpu.SMEM), vmem, vmem],
        out_specs=vmem,
        out_shape=jax.ShapeDtypeStruct((Z_HI, groups, NPROBE, aux_width), BF16),
        scratch_shapes=[pltpu.VMEM((groups, NPROBE, aux_width), F32)],
        compiler_params=pltpu.CompilerParams(vmem_limit_bytes=32 * 2**20),
        name="y_by_owner",
    )(meta, v, tiles)


def everywhere(value, axes):
    count = lax.axis_size(axes)
    copies = jnp.broadcast_to(value[None], (count,) + value.shape)
    return lax.all_to_all(copies, axes, 0, 0)


def mirrored(value):
    z_lo, z_hi = lax.axis_size("z_lo"), lax.axis_size("z_hi")
    pairs = [(i * z_hi + j, (z_lo - 1 - i) * z_hi + (z_hi - 1 - j)) for i in range(z_lo) for j in range(z_hi)]
    return lax.ppermute(value, ("z_lo", "z_hi"), pairs)


def swapped(value):
    return lax.ppermute(value, "core", [(0, 1), (1, 0)])


def body(tiles, atom_of, owner_of, live_count, green, probes):
    tiles = tiles[0, 0]
    slot_count = tiles.shape[0]
    groups = lax.axis_size(AUX)
    meta = jnp.concatenate([owner_of[0, 0], atom_of[0, 0], live_count[0]])
    mine = jnp.swapaxes(green, 1, 2)
    other = swapped(mine)
    probes_all, other = lax.optimization_barrier((everywhere(probes, AUX), other))
    u = make_u(turn(tiles), probes_all, meta, slot_count)
    u = lax.all_to_all(u, AUX, 0, 0)
    near = make_near(u, mine, other)
    far = mirrored(make_far(mirrored(make_rows(u, mine.shape[2])), mine, other))
    v = make_back(u, near, far)
    y = make_y(lax.all_to_all(v, AUX, 0, 0), tiles, meta, groups)
    y = lax.all_to_all(y.reshape((Z_HI * groups,) + y.shape[2:]), OUTER, 0, 0)
    y = jnp.sum(y.astype(F32), axis=0)
    return jnp.sum(everywhere(y, LAST), axis=0)


def solution(mesh):
    aux, orb, rep = mesh.devices.shape
    x = 4
    names = ("z_lo", "x", "z_hi", "core", "rep")
    fine = Mesh(mesh.devices.reshape(aux // x, x, Z_HI, orb // Z_HI, rep), names)
    orbs, atoms = names[2:4], names[2:]
    return jax.shard_map(
        body,
        mesh=fine,
        in_specs=(
            P(AUX, atoms, None, None, None),
            P(AUX, atoms, None),
            P(AUX, atoms, None),
            P(AUX, atoms),
            P(None, None, orbs),
            P(None, AUX),
        ),
        out_specs=P(None, AUX),
        check_vma=False,
    )
```

time: 151 us -> 145 us (0.960)
  blocking collectives: 110 us -> 87.8 us
  starting transfers between devices: 17.9 us -> 28.9 us
  waiting for transfers between devices: 3 us -> 8.65 us
    all_to_all x2, blocking collectives: 73.1 us -> 43.7 us  [the longest x1 23.1 us: body(): u = lax.all_to_all(u, AUX, 0, 0)]
    ppermute x1 -> x3, starting transfers between devices: 12.4 us -> 23.4 us  [the longest x1 12.4 us: swapped(): return lax.ppermute(value, 'core', [(0, 1), (1, 0)])]
    ppermute x1 -> x3, waiting for transfers between devices: 0.01 us -> 5.65 us  [the longest x2 5.65 us: mirrored(): return lax.ppermute(value, ('z_lo', 'z_hi'), pairs)]
    all_to_all x1, blocking collectives: 17.8 us -> 22.7 us  [body(): y = lax.all_to_all(y.reshape((Z_HI * groups,) + y.shape[2:]), OUTER, 0, 0)]
    all_to_all x1, blocking collectives: 19 us -> 21.4 us  [everywhere(): return lax.all_to_all(copies, axes, 0, 0)]
    pallas_call x1 -> x4, Pallas kernels: 5.9 us -> 5.05 us  [on_vmem(): pl.pallas_call(kernel, in_specs=[vmem] * len(args), out_specs=vmem, out_s...]
  transfers between devices with their start and end apart: 2 -> 4, of which waited for: 1 -> 3; matrix products, arithmetic and copies ran while one was open for 1% -> 1% of each run, Pallas kernels for 2% -> 4%
where the time goes in v4:
time: 145 us
  blocking collectives  87.8 us (61%)
  starting transfers between devices  28.9 us (20%)
  Pallas kernels  10.8 us (7%)
  waiting for transfers between devices  8.65 us (6%)
  local copies, waits for them, and re-layouts  7.12 us (5%)
    all_to_all x1, blocking collectives, body(): u = lax.all_to_all(u, AUX, 0, 0)  23.1 us
    all_to_all x1, blocking collectives, body(): y = lax.all_to_all(y.reshape((Z_HI * groups,) + y.shape[2:]), OUTER, 0, 0)  22.7 us
    all_to_all x1, blocking collectives, everywhere(): return lax.all_to_all(copies, axes, 0, 0)  21.4 us
    all_to_all x1, blocking collectives, body(): y = make_y(lax.all_to_all(v, AUX, 0, 0), tiles, meta, groups)  20.7 us
    ppermute x1, starting transfers between devices, swapped(): return lax.ppermute(value, 'core', [(0, 1), (1, 0)])  12.4 us
    ppermute x2, starting transfers between devices, mirrored(): return lax.ppermute(value, ('z_lo', 'z_hi'), pairs)  11 us
    unnamed x14, local copies, waits for them, and re-layouts  5.76 us
    ppermute x2, waiting for transfers between devices, mirrored(): return lax.ppermute(value, ('z_lo', 'z_hi'), pairs)  5.65 us
  transfers between devices with their start and end apart: 4, of which 3 were waited for; matrix products, arithmetic and copies ran while one was open for 1% of the time, Pallas kernels for 4%

profile of v4, /device:TPU:1, one launch (start us, length us, event | category | flops | bytes accessed | tf_op | source)
XLA Modules:
  0.0 144.9 jit_solution(11146969396429944601)
XLA Ops:
  0.0 12.4 %collective-permute-start = (bf16[2,320,1280]{2,1,0:T(8,128)(2,1)}, bf16[2,320,1280]{2,1,0:T(8,128)(2,1)S(1)}, u32[]{:S(2)}, u32[]{:S(2)}) collective-permute-start(bf16[2,320,1280]{2,1,0:T(8,128)(2,1)} %bitcast.9), channel_id=1, source_target_pairs={{0,8},{8,0},{1,9},{9,1},{2,10},{10,2},{3,11},{11,3},{4,12},{12,4},... | collective-permute-start | bytes 4915208 | tf_op jit(solution)/shard_map/ppermute | solution.py:243
  12.4 1.3 broadcast_in_dim.4
  13.8 5.5 %all-to-all-start = ((bf16[24,12,128]{2,1,0:T(8,128)(2,1)}), bf16[24,12,128]{2,1,0:T(8,128)(2,1)S(1)}, u32[]{:S(2)}, u32[]{:S(2)}) async-start(bf16[24,12,128]{2,1,0:T(8,128)(2,1)} %broadcast_in_dim.4), calls=%async_computation | async-start | bytes 196608 | tf_op jit(solution)/shard_map/all_to_all | solution.py:233
  19.9 0.0 copy-start.2
  20.0 1.9 %copy-done.2 = bf16[1,1,8,1600,128]{4,3,2,1,0:T(8,128)(2,1)S(1)} copy-done((bf16[1,1,8,1600,128]{4,3,2,1,0:T(8,128)(2,1)S(1)}, bf16[1,1,8,1600,128]{4,3,2,1,0:T(8,128)(2,1)}, u32[]{:S(2)}) %copy-start.2) | copy-done | bytes 3276824
  21.9 0.0 copy-start.5
  21.9 0.0 copy-start.6
  21.9 0.0 copy-start.4
  21.9 3.1 %turn_tiles.1.turned_ref = bf16[2,1024,800]{2,1,0:T(8,128)(2,1)S(1)} custom-call(bf16[8,1600,128]{2,1,0:T(8,128)(2,1)S(1)} %bitcast.7), custom_call_target="tpu_custom_call" | custom-call | bytes 6553600 | tf_op jit(solution)/shard_map/turn_tiles/pallas_call | solution.py:45
  25.0 0.0 copy-start
  25.0 1.8 %copy-done = bf16[2,1024,800]{2,1,0:T(8,128)(2,1)} copy-done((bf16[2,1024,800]{2,1,0:T(8,128)(2,1)}, bf16[2,1024,800]{2,1,0:T(8,128)(2,1)S(1)}, u32[]{:S(2)}) %copy-start) | copy-done | bytes 3276824
  26.8 0.0 copy-done.5
  26.8 0.0 copy-done.6
  26.8 0.1 pad_add_fusion.meta_ref
  26.9 3.0 %all-to-all-done.probes_ref = bf16[24,12,128]{2,1,0:T(8,128)(2,1)S(1)} async-done(((bf16[24,12,128]{2,1,0:T(8,128)(2,1)}), bf16[24,12,128]{2,1,0:T(8,128)(2,1)S(1)}, u32[]{:S(2)}, u32[]{:S(2)}) %all-to-all-start) | async-done | bytes 73760 | tf_op jit(solution)/shard_map/all_to_all | solution.py:233
  29.9 0.0 collective-permute-done.other_ref
  29.9 0.0 copy-start.1
  29.9 2.0 %copy-done.1 = bf16[2,1024,800]{2,1,0:T(8,128)(2,1)S(1)} copy-done((bf16[2,1024,800]{2,1,0:T(8,128)(2,1)S(1)}, bf16[2,1024,800]{2,1,0:T(8,128)(2,1)}, u32[]{:S(2)}) %copy-start.1) | copy-done | bytes 3276824
  31.9 1.3 u_blocks.1
  33.2 23.1 %all_to_all.25.recv_ref = bf16[24,8,896]{2,1,0:T(8,128)(2,1)S(1)} all-to-all(bf16[24,8,896]{2,1,0:T(8,128)(2,1)S(1)} %u_blocks.1), channel_id=1, replica_groups=mesh['z_lo'=6,'x'=4,'z_hi'=2,'core'=2,'rep'=8] {'z_lo','x'}, dimensions={0} | all-to-all | bytes 688128 | tf_op jit(solution)/shard_map/all_to_all | solution.py:255
  56.3 1.0 u_by_atom.1
  57.2 8.2 %collective-permute-start.1 = (bf16[20,1280]{1,0:T(8,128)(2,1)S(1)}, bf16[20,1280]{1,0:T(8,128)(2,1)S(1)}, u32[]{:S(2)}, u32[]{:S(2)}) collective-permute-start(bf16[20,1280]{1,0:T(8,128)(2,1)S(1)} %u_by_atom.1), channel_id=1, source_target_pairs={{0,656},{16,640},{128,528},{144,512},{256,400},{272,384},{384,272}... | collective-permute-start | bytes 153608 | tf_op jit(solution)/shard_map/ppermute | solution.py:239
  65.4 4.3 %collective-permute-done.1.rows_ref = bf16[20,1280]{1,0:T(8,128)(2,1)S(1)} collective-permute-done((bf16[20,1280]{1,0:T(8,128)(2,1)S(1)}, bf16[20,1280]{1,0:T(8,128)(2,1)S(1)}, u32[]{:S(2)}, u32[]{:S(2)}) %collective-permute-start.1) | collective-permute-done | bytes 51232 | tf_op jit(solution)/shard_map/ppermute | solution.py:239
  69.7 0.0 copy-done.4
  69.7 0.9 v_far.1
  70.6 0.0 copy-start.3
  70.6 2.8 %collective-permute-start.2 = (bf16[20,1280]{1,0:T(8,128)(2,1)S(1)}, bf16[20,1280]{1,0:T(8,128)(2,1)S(1)}, u32[]{:S(2)}, u32[]{:S(2)}) collective-permute-start(bf16[20,1280]{1,0:T(8,128)(2,1)S(1)} %v_far.1), channel_id=1, source_target_pairs={{0,656},{16,640},{128,528},{144,512},{256,400},{272,384},{384,272}... | collective-permute-start | bytes 153608 | tf_op jit(solution)/shard_map/ppermute | solution.py:239
  73.4 2.3 %v_near.1.near_ref = f32[20,1280]{1,0:T(8,128)S(1)} custom-call(bf16[24,8,896]{2,1,0:T(8,128)(2,1)S(1)} %all_to_all.25.recv_ref, bf16[2,320,1280]{2,1,0:T(8,128)(2,1)S(1)} %bitcast.11, bf16[2,320,1280]{2,1,0:T(8,128)(2,1)S(1)} %collective-permute-done.other_ref), custom_call_target="tpu_custom_call" | custom-call | tf_op jit(solution)/shard_map/v_near/pallas_call | solution.py:166
  75.7 1.4 collective-permute-done.2.far_ref
  77.0 0.9 v_back.1
  78.0 20.7 %all_to_all.26.v_ref = bf16[24,8,800]{2,1,0:T(8,128)(2,1)S(1)} all-to-all(bf16[24,8,800]{2,1,0:T(8,128)(2,1)S(1)} %v_back.1), channel_id=1, replica_groups=mesh['z_lo'=6,'x'=4,'z_hi'=2,'core'=2,'rep'=8] {'z_lo','x'}, dimensions={0} | all-to-all | bytes 614400 | tf_op jit(solution)/shard_map/all_to_all | solution.py:259
  98.7 0.0 copy-done.3
  98.7 1.4 y_by_owner.1
  100.0 22.7 %all_to_all.27 = bf16[48,12,128]{2,1,0:T(8,128)(2,1)S(1)} all-to-all(bf16[48,12,128]{2,1,0:T(8,128)(2,1)S(1)} %bitcast.12), channel_id=1, replica_groups=mesh['z_lo'=6,'x'=4,'z_hi'=2,'core'=2,'rep'=8] {'z_hi','z_lo','x'}, dimensions={0} | all-to-all | bytes 294912 | tf_op jit(solution)/shard_map/all_to_all | solution.py:260
  122.8 0.1 convert_reduce_fusion
  122.8 21.4 %all_to_all.28 = f32[16,12,128]{2,1,0:T(8,128)S(1)} all-to-all(f32[16,12,128]{2,1,0:T(8,128)S(1)} %broadcast_in_dim.5), channel_id=1, replica_groups=mesh['z_lo'=6,'x'=4,'z_hi'=2,'core'=2,'rep'=8] {'core','rep'}, dimensions={0} | all-to-all | bytes 196608 | tf_op jit(solution)/shard_map/all_to_all | solution.py:233
  144.2 0.6 reduce_sum.19
  (1 shorter events, 0.0 us)
Async XLA Ops:
  0.0 29.9 %collective-permute-start = (bf16[2,320,1280]{2,1,0:T(8,128)(2,1)}, bf16[2,320,1280]{2,1,0:T(8,128)(2,1)S(1)}, u32[]{:S(2)}, u32[]{:S(2)}) collective-permute-start(bf16[2,320,1280]{2,1,0:T(8,128)(2,1)} %bitcast.9), channel_id=1, source_target_pairs={{0,8},{8,0},{1,9},{9,1},{2,10},{10,2},{3,11},{11,3},{4,12},{12,4},... | collective-permute-start | bytes 4915208 | tf_op jit(solution)/shard_map/ppermute | solution.py:243
  13.8 16.1 %all-to-all-start = ((bf16[24,12,128]{2,1,0:T(8,128)(2,1)}), bf16[24,12,128]{2,1,0:T(8,128)(2,1)S(1)}, u32[]{:S(2)}, u32[]{:S(2)}) async-start(bf16[24,12,128]{2,1,0:T(8,128)(2,1)} %broadcast_in_dim.4), calls=%async_computation | async-start | bytes 196608 | tf_op jit(solution)/shard_map/all_to_all | solution.py:233
  19.9 1.9 %copy-start.2 = (bf16[1,1,8,1600,128]{4,3,2,1,0:T(8,128)(2,1)S(1)}, bf16[1,1,8,1600,128]{4,3,2,1,0:T(8,128)(2,1)}, u32[]{:S(2)}) copy-start(bf16[1,1,8,1600,128]{4,3,2,1,0:T(8,128)(2,1)} %param.6) | copy-start | bytes 9830404
  21.9 4.9 %copy-start.5 = (s32[1,1,8]{2,1,0:T(1,128)S(1)}, s32[1,1,8]{2,1,0:T(1,128)}, u32[]{:S(2)}) copy-start(s32[1,1,8]{2,1,0:T(1,128)} %param.7) | copy-start | bytes 100
  21.9 4.9 %copy-start.6 = (s32[1,1,8]{2,1,0:T(1,128)S(1)}, s32[1,1,8]{2,1,0:T(1,128)}, u32[]{:S(2)}) copy-start(s32[1,1,8]{2,1,0:T(1,128)} %param.8) | copy-start | bytes 100
  21.9 47.8 %copy-start.4 = (bf16[2,1280,320]{1,2,0:T(8,128)(2,1)S(1)}, bf16[2,1280,320]{1,2,0:T(8,128)(2,1)}, u32[]{:S(2)}) copy-start(bf16[2,1280,320]{1,2,0:T(8,128)(2,1)} %param.10) | copy-start | bytes 4915204
  25.0 1.8 %copy-start = (bf16[2,1024,800]{2,1,0:T(8,128)(2,1)}, bf16[2,1024,800]{2,1,0:T(8,128)(2,1)S(1)}, u32[]{:S(2)}) copy-start(bf16[2,1024,800]{2,1,0:T(8,128)(2,1)S(1)} %turn_tiles.1.turned_ref) | copy-start | bytes 9830404
  29.9 2.0 %copy-start.1 = (bf16[2,1024,800]{2,1,0:T(8,128)(2,1)S(1)}, bf16[2,1024,800]{2,1,0:T(8,128)(2,1)}, u32[]{:S(2)}) copy-start(bf16[2,1024,800]{2,1,0:T(8,128)(2,1)} %copy-done) | copy-start | bytes 9830404
  57.2 12.5 %collective-permute-start.1 = (bf16[20,1280]{1,0:T(8,128)(2,1)S(1)}, bf16[20,1280]{1,0:T(8,128)(2,1)S(1)}, u32[]{:S(2)}, u32[]{:S(2)}) collective-permute-start(bf16[20,1280]{1,0:T(8,128)(2,1)S(1)} %u_by_atom.1), channel_id=1, source_target_pairs={{0,656},{16,640},{128,528},{144,512},{256,400},{272,384},{384,272}... | collective-permute-start | bytes 153608 | tf_op jit(solution)/shard_map/ppermute | solution.py:239
  70.6 28.1 %copy-start.3 = (bf16[1,1,8,1600,128]{4,3,2,1,0:T(8,128)(2,1)S(1)}, bf16[1,1,8,1600,128]{4,3,2,1,0:T(8,128)(2,1)}, u32[]{:S(2)}) copy-start(bf16[1,1,8,1600,128]{4,3,2,1,0:T(8,128)(2,1)} %param.6) | copy-start | bytes 9830404
  70.6 6.4 %collective-permute-start.2 = (bf16[20,1280]{1,0:T(8,128)(2,1)S(1)}, bf16[20,1280]{1,0:T(8,128)(2,1)S(1)}, u32[]{:S(2)}, u32[]{:S(2)}) collective-permute-start(bf16[20,1280]{1,0:T(8,128)(2,1)S(1)} %v_far.1), channel_id=1, source_target_pairs={{0,656},{16,640},{128,528},{144,512},{256,400},{272,384},{384,272}... | collective-permute-start | bytes 153608 | tf_op jit(solution)/shard_map/ppermute | solution.py:239

commit v5 on v4

--- a/solution.py
+++ b/solution.py
@@ -108,10 +108,11 @@
 def through(rows, panels):
     v = None
     for panel in panels:
-        w = dot(rows, panel[1], 1, 1)
+        occ, vir = panel[0][...], panel[1][...]
+        w = dot(rows, vir, 1, 1)
         if w.shape[0] > SIG:
             w = w[:SIG] + w[SIG:]
-        part = dot(w.astype(BF16), panel[0], 1, 0)
+        part = dot(w.astype(BF16), occ, 1, 0)
         v = part if v is None else v + part
     return v
 
@@ -140,12 +141,12 @@
     rows_ref[...] = by_atom(recv_ref, rows_ref.shape[1], False)
 
 
-def near_kernel(recv_ref, mine_ref, other_ref, out_ref):
-    out_ref[...] = through(by_atom(recv_ref, out_ref.shape[1], True), (mine_ref, other_ref))
-
-
-def far_kernel(rows_ref, mine_ref, other_ref, out_ref):
-    out_ref[...] = through(rows_ref[...], (mine_ref, other_ref)).astype(BF16)
+def near_kernel(recv_ref, mine_ref, occ_ref, vir_ref, out_ref):
+    out_ref[...] = through(by_atom(recv_ref, out_ref.shape[1], True), ((mine_ref.at[0], mine_ref.at[1]), (occ_ref, vir_ref)))
+
+
+def far_kernel(rows_ref, mine_ref, occ_ref, vir_ref, out_ref):
+    out_ref[...] = through(rows_ref[...], ((mine_ref.at[0], mine_ref.at[1]), (occ_ref, vir_ref))).astype(BF16)
 
 
 def back_kernel(recv_ref, near_ref, far_ref, out_ref):
@@ -177,13 +178,13 @@
     return on_vmem(sum_kernel, jax.ShapeDtypeStruct((SIG, orb), BF16), "u_by_atom", recv)
 
 
-def make_near(recv, mine, other):
+def make_near(recv, mine, occ, vir):
     shape = jax.ShapeDtypeStruct((SIG, mine.shape[2]), F32)
-    return on_vmem(near_kernel, shape, "v_near", recv, mine, other)
-
-
-def make_far(rows, mine, other):
-    return on_vmem(far_kernel, jax.ShapeDtypeStruct(rows.shape, BF16), "v_far", rows, mine, other)
+    return on_vmem(near_kernel, shape, "v_near", recv, mine, occ, vir)
+
+
+def make_far(rows, mine, occ, vir):
+    return on_vmem(far_kernel, jax.ShapeDtypeStruct(rows.shape, BF16), "v_far", rows, mine, occ, vir)
 
 
 def make_back(recv, near, far):
@@ -233,9 +234,9 @@
     return lax.all_to_all(copies, axes, 0, 0)
 
 
-def mirrored(value):
+def beyond(value):
     z_lo, z_hi = lax.axis_size("z_lo"), lax.axis_size("z_hi")
-    pairs = [(i * z_hi + j, (z_lo - 1 - i) * z_hi + (z_hi - 1 - j)) for i in range(z_lo) for j in range(z_hi)]
+    pairs = [(i * z_hi + j, (i + z_lo // 2) % z_lo * z_hi + (z_hi - 1 - j)) for i in range(z_lo) for j in range(z_hi)]
     return lax.ppermute(value, ("z_lo", "z_hi"), pairs)
 
 
@@ -249,17 +250,17 @@
     groups = lax.axis_size(AUX)
     meta = jnp.concatenate([owner_of[0, 0], atom_of[0, 0], live_count[0]])
     mine = jnp.swapaxes(green, 1, 2)
-    other = swapped(mine)
-    probes_all, other = lax.optimization_barrier((everywhere(probes, AUX), other))
+    vir, occ = swapped(mine[1]), swapped(mine[0])
+    probes_all = everywhere(probes, AUX)
     u = make_u(turn(tiles), probes_all, meta, slot_count)
-    u = lax.all_to_all(u, AUX, 0, 0)
-    near = make_near(u, mine, other)
-    far = mirrored(make_far(mirrored(make_rows(u, mine.shape[2])), mine, other))
+    u, vir, occ = lax.optimization_barrier((lax.all_to_all(u, AUX, 0, 0), vir, occ))
+    near = make_near(u, mine, occ, vir)
+    far = beyond(make_far(beyond(make_rows(u, mine.shape[2])), mine, occ, vir))
     v = make_back(u, near, far)
     y = make_y(lax.all_to_all(v, AUX, 0, 0), tiles, meta, groups)
     y = lax.all_to_all(y.reshape((Z_HI * groups,) + y.shape[2:]), OUTER, 0, 0)
-    y = jnp.sum(y.astype(F32), axis=0)
-    return jnp.sum(everywhere(y, LAST), axis=0)
+    y = jnp.sum(y.astype(F32), axis=0).astype(BF16)
+    return jnp.sum(everywhere(y, LAST).astype(F32), axis=0)
 
 
 def solution(mesh):

time: 145 us -> 142 us (0.979)
  blocking collectives: 87.8 us -> 61.5 us
  starting transfers between devices: 28.9 us -> 43.1 us
  waiting for transfers between devices: 8.65 us -> 14.2 us
  local copies, waits for them, and re-layouts: 7.12 us -> 9.29 us
    all_to_all x1 -> x0, blocking collectives: 23.1 us -> none  [body(): u = lax.all_to_all(u, AUX, 0, 0)]
    all_to_all x1, starting transfers between devices: 5.51 us -> 15.4 us  [everywhere(): return lax.all_to_all(copies, axes, 0, 0)]
    all_to_all x0 -> x1, starting transfers between devices: none -> 7.57 us  [body(): lax.all_to_all(u, AUX, 0, 0)]
    all_to_all x0 -> x1, waiting for transfers between devices: none -> 7.47 us  [body(): lax.all_to_all(u, AUX, 0, 0)]
    ppermute x1 -> x2, starting transfers between devices: 12.4 us -> 5.35 us  [swapped(): return lax.ppermute(value, 'core', [(0, 1), (1, 0)])]
    ppermute x2, waiting for transfers between devices: 5.65 us -> 1.81 us  [beyond(): return lax.ppermute(value, ('z_lo', 'z_hi'), pairs)]
    ppermute x2, starting transfers between devices: 11 us -> 14.8 us  [beyond(): return lax.ppermute(value, ('z_lo', 'z_hi'), pairs)]
    ppermute x1 -> x2, waiting for transfers between devices: 0.01 us -> 2.3 us  [swapped(): return lax.ppermute(value, 'core', [(0, 1), (1, 0)])]
  transfers between devices with their start and end apart: 4 -> 6, of which waited for: 3 -> 4; matrix products, arithmetic and copies ran while one was open for 1% -> 0% of each run, Pallas kernels for 4% -> 4%
where the time goes in v5:
time: 142 us; the launch traced here: 141 us
  blocking collectives  61.5 us (43%)
  starting transfers between devices  43.1 us (30%)
  waiting for transfers between devices  14.2 us (10%)
  Pallas kernels  11.6 us (8%)
  local copies, waits for them, and re-layouts  9.29 us (7%)
    all_to_all x1, blocking collectives, everywhere(): return lax.all_to_all(copies, axes, 0, 0)  20.9 us
    all_to_all x1, blocking collectives, body(): y = lax.all_to_all(y.reshape((Z_HI * groups,) + y.shape[2:]), OUTER, 0, 0)  20.5 us
    all_to_all x1, blocking collectives, body(): y = make_y(lax.all_to_all(v, AUX, 0, 0), tiles, meta, groups)  20.1 us
    all_to_all x1, starting transfers between devices, everywhere(): return lax.all_to_all(copies, axes, 0, 0)  15.4 us
    ppermute x2, starting transfers between devices, beyond(): return lax.ppermute(value, ('z_lo', 'z_hi'), pairs)  14.8 us
    unnamed x18, local copies, waits for them, and re-layouts  7.83 us
    all_to_all x1, starting transfers between devices, body(): lax.all_to_all(u, AUX, 0, 0)  7.57 us
    all_to_all x1, waiting for transfers between devices, body(): lax.all_to_all(u, AUX, 0, 0)  7.47 us
  transfers between devices with their start and end apart: 6, of which 4 were waited for; matrix products, arithmetic and copies ran while one was open for 0% of the time, Pallas kernels for 4%

profile of v5, /device:TPU:1, one launch (start us, length us, event | category | flops | bytes accessed | tf_op | source)
XLA Modules:
  0.0 141.2 jit_solution(5319108071895403176)
XLA Ops:
  0.0 1.3 broadcast_in_dim.4
  1.3 15.4 %all-to-all-start = ((bf16[24,12,128]{2,1,0:T(8,128)(2,1)}), bf16[24,12,128]{2,1,0:T(8,128)(2,1)S(1)}, u32[]{:S(2)}, u32[]{:S(2)}) async-start(bf16[24,12,128]{2,1,0:T(8,128)(2,1)} %broadcast_in_dim.4), calls=%async_computation | async-start | bytes 196608 | tf_op jit(solution)/shard_map/all_to_all | solution.py:234
  17.3 0.0 copy-start.3
  17.4 1.9 %copy-done.3 = bf16[1,1,8,1600,128]{4,3,2,1,0:T(8,128)(2,1)S(1)} copy-done((bf16[1,1,8,1600,128]{4,3,2,1,0:T(8,128)(2,1)S(1)}, bf16[1,1,8,1600,128]{4,3,2,1,0:T(8,128)(2,1)}, u32[]{:S(2)}) %copy-start.3) | copy-done | bytes 3276824
  19.3 0.0 copy-start.7
  19.3 0.0 copy-start.8
  19.3 3.1 %turn_tiles.1.turned_ref = bf16[2,1024,800]{2,1,0:T(8,128)(2,1)S(1)} custom-call(bf16[8,1600,128]{2,1,0:T(8,128)(2,1)S(1)} %bitcast.14), custom_call_target="tpu_custom_call" | custom-call | bytes 6553600 | tf_op jit(solution)/shard_map/turn_tiles/pallas_call | solution.py:45
  22.4 0.0 copy-start.1
  22.4 1.8 %copy-done.1 = bf16[2,1024,800]{2,1,0:T(8,128)(2,1)} copy-done((bf16[2,1024,800]{2,1,0:T(8,128)(2,1)}, bf16[2,1024,800]{2,1,0:T(8,128)(2,1)S(1)}, u32[]{:S(2)}) %copy-start.1) | copy-done | bytes 3276824
  24.2 0.0 copy-start
  24.2 0.0 copy-done.7
  24.2 0.0 copy-done.8
  24.2 0.1 pad_add_fusion.meta_ref
  24.3 2.6 %all-to-all-done.probes_ref = bf16[24,12,128]{2,1,0:T(8,128)(2,1)S(1)} async-done(((bf16[24,12,128]{2,1,0:T(8,128)(2,1)}), bf16[24,12,128]{2,1,0:T(8,128)(2,1)S(1)}, u32[]{:S(2)}, u32[]{:S(2)}) %all-to-all-start) | async-done | bytes 73760 | tf_op jit(solution)/shard_map/all_to_all | solution.py:234
  26.9 0.0 copy-start.2
  26.9 2.0 %copy-done.2 = bf16[2,1024,800]{2,1,0:T(8,128)(2,1)S(1)} copy-done((bf16[2,1024,800]{2,1,0:T(8,128)(2,1)S(1)}, bf16[2,1024,800]{2,1,0:T(8,128)(2,1)}, u32[]{:S(2)}) %copy-start.2) | copy-done | bytes 3276824
  28.9 2.0 %u_blocks.1 = bf16[24,8,896]{2,1,0:T(8,128)(2,1)} custom-call(s32[17]{0:T(128)S(1)} %pad_add_fusion.meta_ref, bf16[24,12,128]{2,1,0:T(8,128)(2,1)S(1)} %all-to-all-done.probes_ref, bf16[2,1024,800]{2,1,0:T(8,128)(2,1)S(1)} %copy-done.2), custom_call_target="tpu_custom_call" | custom-call | tf_op jit(solution)/shard_map/u_blocks/pallas_call | solution.py:87
  30.9 7.6 %all-to-all-start.1 = ((bf16[24,8,896]{2,1,0:T(8,128)(2,1)}), bf16[24,8,896]{2,1,0:T(8,128)(2,1)S(1)}, u32[]{:S(2)}, u32[]{:S(2)}) async-start(bf16[24,8,896]{2,1,0:T(8,128)(2,1)} %u_blocks.1), calls=%async_computation.1 | async-start | bytes 688128 | tf_op jit(solution)/shard_map/all_to_all | solution.py:256
  38.5 0.0 copy-done
  38.5 0.1 slice_bitcast_fusion
  38.7 3.4 %collective-permute-start = (bf16[320,1280]{1,0:T(8,128)(2,1)S(1)}, bf16[320,1280]{1,0:T(8,128)(2,1)S(1)}, u32[]{:S(2)}, u32[]{:S(2)}) collective-permute-start(bf16[320,1280]{1,0:T(8,128)(2,1)S(1)} %get-tuple-element.12), channel_id=1, source_target_pairs={{0,8},{8,0},{1,9},{9,1},{2,10},{10,2},{3,11},{11,3},{4,12},{12,4},... | collective-permute-start | bytes 2457608 | tf_op jit(solution)/shard_map/ppermute | solution.py:244
  42.1 1.9 %collective-permute-start.1 = (bf16[320,1280]{1,0:T(8,128)(2,1)S(1)}, bf16[320,1280]{1,0:T(8,128)(2,1)S(1)}, u32[]{:S(2)}, u32[]{:S(2)}) collective-permute-start(bf16[320,1280]{1,0:T(8,128)(2,1)S(1)} %get-tuple-element.11), channel_id=1, source_target_pairs={{0,8},{8,0},{1,9},{9,1},{2,10},{10,2},{3,11},{11,3},{4,12},{12,4},... | collective-permute-start | bytes 2457608 | tf_op jit(solution)/shard_map/ppermute | solution.py:244
  44.0 0.0 collective-permute-done.vir_ref
  44.0 2.3 %collective-permute-done.1.occ_ref = bf16[320,1280]{1,0:T(8,128)(2,1)S(1)} collective-permute-done((bf16[320,1280]{1,0:T(8,128)(2,1)S(1)}, bf16[320,1280]{1,0:T(8,128)(2,1)S(1)}, u32[]{:S(2)}, u32[]{:S(2)}) %collective-permute-start.1) | collective-permute-done | bytes 819232 | tf_op jit(solution)/shard_map/ppermute | solution.py:244
  46.3 0.0 copy-start.5
  46.3 0.9 copy-done.5
  47.2 7.5 %all-to-all-done.1.recv_ref = bf16[24,8,896]{2,1,0:T(8,128)(2,1)S(1)} async-done(((bf16[24,8,896]{2,1,0:T(8,128)(2,1)}), bf16[24,8,896]{2,1,0:T(8,128)(2,1)S(1)}, u32[]{:S(2)}, u32[]{:S(2)}) %all-to-all-start.1) | async-done | bytes 344096 | tf_op jit(solution)/shard_map/all_to_all | solution.py:256
  54.7 1.0 u_by_atom.1
  55.7 7.7 %collective-permute-start.2 = (bf16[20,1280]{1,0:T(8,128)(2,1)S(1)}, bf16[20,1280]{1,0:T(8,128)(2,1)S(1)}, u32[]{:S(2)}, u32[]{:S(2)}) collective-permute-start(bf16[20,1280]{1,0:T(8,128)(2,1)S(1)} %u_by_atom.1), channel_id=1, source_target_pairs={{0,400},{16,384},{128,528},{144,512},{256,656},{272,640},{384,16},... | collective-permute-start | bytes 153608 | tf_op jit(solution)/shard_map/ppermute | solution.py:240
  63.4 1.8 %collective-permute-done.2.rows_ref = bf16[20,1280]{1,0:T(8,128)(2,1)S(1)} collective-permute-done((bf16[20,1280]{1,0:T(8,128)(2,1)S(1)}, bf16[20,1280]{1,0:T(8,128)(2,1)S(1)}, u32[]{:S(2)}, u32[]{:S(2)}) %collective-permute-start.2) | collective-permute-done | bytes 51232 | tf_op jit(solution)/shard_map/ppermute | solution.py:240
  65.2 0.0 copy-start.6
  65.2 1.1 copy-done.6
  66.4 0.9 v_far.1
  67.2 0.0 copy-start.4
  67.2 7.1 %collective-permute-start.3 = (bf16[20,1280]{1,0:T(8,128)(2,1)S(1)}, bf16[20,1280]{1,0:T(8,128)(2,1)S(1)}, u32[]{:S(2)}, u32[]{:S(2)}) collective-permute-start(bf16[20,1280]{1,0:T(8,128)(2,1)S(1)} %v_far.1), channel_id=1, source_target_pairs={{0,400},{16,384},{128,528},{144,512},{256,656},{272,640},{384,16},... | collective-permute-start | bytes 153608 | tf_op jit(solution)/shard_map/ppermute | solution.py:240
  74.3 2.3 %v_near.1.near_ref = f32[20,1280]{1,0:T(8,128)S(1)} custom-call(bf16[24,8,896]{2,1,0:T(8,128)(2,1)S(1)} %all-to-all-done.1.recv_ref, bf16[2,320,1280]{2,1,0:T(8,128)(2,1)S(1)} %bitcast.13, bf16[320,1280]{1,0:T(8,128)(2,1)S(1)} %copy-done.6, bf16[320,1280]{1,0:T(8,128)(2,1)S(1)} %collective-permute-done.vir_ref), custom_call_target="tpu_custom_call" | custom-call | tf_op jit(solution)/shard_map/v_near/pallas_call | solution.py:167
  76.6 0.0 collective-permute-done.3.far_ref
  76.6 1.0 v_back.1
  77.6 20.1 %all_to_all.25.v_ref = bf16[24,8,800]{2,1,0:T(8,128)(2,1)S(1)} all-to-all(bf16[24,8,800]{2,1,0:T(8,128)(2,1)S(1)} %v_back.1), channel_id=1, replica_groups=mesh['z_lo'=6,'x'=4,'z_hi'=2,'core'=2,'rep'=8] {'z_lo','x'}, dimensions={0} | all-to-all | bytes 614400 | tf_op jit(solution)/shard_map/all_to_all | solution.py:260
  97.7 0.0 copy-done.4
  97.7 1.4 y_by_owner.1
  99.1 20.5 %all_to_all.26 = bf16[48,12,128]{2,1,0:T(8,128)(2,1)S(1)} all-to-all(bf16[48,12,128]{2,1,0:T(8,128)(2,1)S(1)} %bitcast.16), channel_id=1, replica_groups=mesh['z_lo'=6,'x'=4,'z_hi'=2,'core'=2,'rep'=8] {'z_hi','z_lo','x'}, dimensions={0} | all-to-all | bytes 294912 | tf_op jit(solution)/shard_map/all_to_all | solution.py:261
  119.5 0.1 reduce_sum.21
  119.6 20.9 %all_to_all.27 = bf16[16,12,128]{2,1,0:T(8,128)(2,1)S(1)} all-to-all(bf16[16,12,128]{2,1,0:T(8,128)(2,1)S(1)} %broadcast_in_dim.5), channel_id=1, replica_groups=mesh['z_lo'=6,'x'=4,'z_hi'=2,'core'=2,'rep'=8] {'core','rep'}, dimensions={0} | all-to-all | bytes 98304 | tf_op jit(solution)/shard_map/all_to_all | solution.py:234
  140.6 0.6 convert_reduce_fusion
  (1 shorter events, 0.0 us)
Async XLA Ops:
  1.3 25.5 %all-to-all-start = ((bf16[24,12,128]{2,1,0:T(8,128)(2,1)}), bf16[24,12,128]{2,1,0:T(8,128)(2,1)S(1)}, u32[]{:S(2)}, u32[]{:S(2)}) async-start(bf16[24,12,128]{2,1,0:T(8,128)(2,1)} %broadcast_in_dim.4), calls=%async_computation | async-start | bytes 196608 | tf_op jit(solution)/shard_map/all_to_all | solution.py:234
  17.3 1.9 %copy-start.3 = (bf16[1,1,8,1600,128]{4,3,2,1,0:T(8,128)(2,1)S(1)}, bf16[1,1,8,1600,128]{4,3,2,1,0:T(8,128)(2,1)}, u32[]{:S(2)}) copy-start(bf16[1,1,8,1600,128]{4,3,2,1,0:T(8,128)(2,1)} %param.6) | copy-start | bytes 9830404
  19.3 4.9 %copy-start.7 = (s32[1,1,8]{2,1,0:T(1,128)S(1)}, s32[1,1,8]{2,1,0:T(1,128)}, u32[]{:S(2)}) copy-start(s32[1,1,8]{2,1,0:T(1,128)} %param.7) | copy-start | bytes 100
  19.3 4.9 %copy-start.8 = (s32[1,1,8]{2,1,0:T(1,128)S(1)}, s32[1,1,8]{2,1,0:T(1,128)}, u32[]{:S(2)}) copy-start(s32[1,1,8]{2,1,0:T(1,128)} %param.8) | copy-start | bytes 100
  22.4 1.8 %copy-start.1 = (bf16[2,1024,800]{2,1,0:T(8,128)(2,1)}, bf16[2,1024,800]{2,1,0:T(8,128)(2,1)S(1)}, u32[]{:S(2)}) copy-start(bf16[2,1024,800]{2,1,0:T(8,128)(2,1)S(1)} %turn_tiles.1.turned_ref) | copy-start | bytes 9830404
  24.2 14.3 %copy-start = (bf16[2,1280,320]{1,2,0:T(8,128)(2,1)S(1)}, bf16[2,1280,320]{1,2,0:T(8,128)(2,1)}, u32[]{:S(2)}) copy-start(bf16[2,1280,320]{1,2,0:T(8,128)(2,1)} %param.10) | copy-start | bytes 4915204
  26.9 2.0 %copy-start.2 = (bf16[2,1024,800]{2,1,0:T(8,128)(2,1)S(1)}, bf16[2,1024,800]{2,1,0:T(8,128)(2,1)}, u32[]{:S(2)}) copy-start(bf16[2,1024,800]{2,1,0:T(8,128)(2,1)} %copy-done.1) | copy-start | bytes 9830404
  30.9 23.8 %all-to-all-start.1 = ((bf16[24,8,896]{2,1,0:T(8,128)(2,1)}), bf16[24,8,896]{2,1,0:T(8,128)(2,1)S(1)}, u32[]{:S(2)}, u32[]{:S(2)}) async-start(bf16[24,8,896]{2,1,0:T(8,128)(2,1)} %u_blocks.1), calls=%async_computation.1 | async-start | bytes 688128 | tf_op jit(solution)/shard_map/all_to_all | solution.py:256
  38.7 5.4 %collective-permute-start = (bf16[320,1280]{1,0:T(8,128)(2,1)S(1)}, bf16[320,1280]{1,0:T(8,128)(2,1)S(1)}, u32[]{:S(2)}, u32[]{:S(2)}) collective-permute-start(bf16[320,1280]{1,0:T(8,128)(2,1)S(1)} %get-tuple-element.12), channel_id=1, source_target_pairs={{0,8},{8,0},{1,9},{9,1},{2,10},{10,2},{3,11},{11,3},{4,12},{12,4},... | collective-permute-start | bytes 2457608 | tf_op jit(solution)/shard_map/ppermute | solution.py:244
  42.1 4.2 %collective-permute-start.1 = (bf16[320,1280]{1,0:T(8,128)(2,1)S(1)}, bf16[320,1280]{1,0:T(8,128)(2,1)S(1)}, u32[]{:S(2)}, u32[]{:S(2)}) collective-permute-start(bf16[320,1280]{1,0:T(8,128)(2,1)S(1)} %get-tuple-element.11), channel_id=1, source_target_pairs={{0,8},{8,0},{1,9},{9,1},{2,10},{10,2},{3,11},{11,3},{4,12},{12,4},... | collective-permute-start | bytes 2457608 | tf_op jit(solution)/shard_map/ppermute | solution.py:244
  46.3 0.9 copy-start.5
  55.7 9.6 %collective-permute-start.2 = (bf16[20,1280]{1,0:T(8,128)(2,1)S(1)}, bf16[20,1280]{1,0:T(8,128)(2,1)S(1)}, u32[]{:S(2)}, u32[]{:S(2)}) collective-permute-start(bf16[20,1280]{1,0:T(8,128)(2,1)S(1)} %u_by_atom.1), channel_id=1, source_target_pairs={{0,400},{16,384},{128,528},{144,512},{256,656},{272,640},{384,16},... | collective-permute-start | bytes 153608 | tf_op jit(solution)/shard_map/ppermute | solution.py:240
  65.2 1.1 copy-start.6
  67.2 30.5 %copy-start.4 = (bf16[1,1,8,1600,128]{4,3,2,1,0:T(8,128)(2,1)S(1)}, bf16[1,1,8,1600,128]{4,3,2,1,0:T(8,128)(2,1)}, u32[]{:S(2)}) copy-start(bf16[1,1,8,1600,128]{4,3,2,1,0:T(8,128)(2,1)} %param.6) | copy-start | bytes 9830404
  67.2 9.4 %collective-permute-start.3 = (bf16[20,1280]{1,0:T(8,128)(2,1)S(1)}, bf16[20,1280]{1,0:T(8,128)(2,1)S(1)}, u32[]{:S(2)}, u32[]{:S(2)}) collective-permute-start(bf16[20,1280]{1,0:T(8,128)(2,1)S(1)} %v_far.1), channel_id=1, source_target_pairs={{0,400},{16,384},{128,528},{144,512},{256,656},{272,640},{384,16},... | collective-permute-start | bytes 153608 | tf_op jit(solution)/shard_map/ppermute | solution.py:240

commit v6 on v5

--- a/solution.py
+++ b/solution.py
@@ -129,12 +129,12 @@
 
     def by_row(part):
         full = dot(part, copies, 1, 0).reshape(SIG, atoms, orb)
-        return jnp.sum(jnp.where(own_atom[None], full, 0.0), axis=1).astype(BF16)
+        return jnp.sum(jnp.where(own_atom[None], full, 0.0), axis=1)
 
     if not rest:
-        return by_row(high)
+        return by_row(high).astype(BF16)
     low = (stacked - high.astype(F32)).astype(BF16)
-    return jnp.concatenate([by_row(high), by_row(low)], axis=0)
+    return jnp.concatenate([by_row(high), by_row(low)], axis=0).astype(BF16)
 
 
 def sum_kernel(recv_ref, rows_ref):

time: 142 us -> 142 us (level)
  no operation moved by 1% of the time
where the time goes in v6:
time: 142 us; the launch traced here: 141 us
  blocking collectives  61.6 us (43%)
  starting transfers between devices  43.1 us (30%)
  waiting for transfers between devices  14.2 us (10%)
  Pallas kernels  11.5 us (8%)
  local copies, waits for them, and re-layouts  9.29 us (7%)
    all_to_all x1, blocking collectives, everywhere(): return lax.all_to_all(copies, axes, 0, 0)  21 us
    all_to_all x1, blocking collectives, body(): y = lax.all_to_all(y.reshape((Z_HI * groups,) + y.shape[2:]), OUTER, 0, 0)  20.5 us
    all_to_all x1, blocking collectives, body(): y = make_y(lax.all_to_all(v, AUX, 0, 0), tiles, meta, groups)  20.2 us
    all_to_all x1, starting transfers between devices, everywhere(): return lax.all_to_all(copies, axes, 0, 0)  15.4 us
    ppermute x2, starting transfers between devices, beyond(): return lax.ppermute(value, ('z_lo', 'z_hi'), pairs)  14.8 us
    unnamed x18, local copies, waits for them, and re-layouts  7.83 us
    all_to_all x1, starting transfers between devices, body(): lax.all_to_all(u, AUX, 0, 0)  7.57 us
    all_to_all x1, waiting for transfers between devices, body(): lax.all_to_all(u, AUX, 0, 0)  7.49 us
  transfers between devices with their start and end apart: 6, of which 4 were waited for; matrix products, arithmetic and copies ran while one was open for 0% of the time, Pallas kernels for 4%

profile of v6, /device:TPU:1, one launch (start us, length us, event | category | flops | bytes accessed | tf_op | source)
XLA Modules:
  0.0 141.2 jit_solution(12418672408534080839)
XLA Ops:
  0.0 1.3 broadcast_in_dim.4
  1.3 15.4 %all-to-all-start = ((bf16[24,12,128]{2,1,0:T(8,128)(2,1)}), bf16[24,12,128]{2,1,0:T(8,128)(2,1)S(1)}, u32[]{:S(2)}, u32[]{:S(2)}) async-start(bf16[24,12,128]{2,1,0:T(8,128)(2,1)} %broadcast_in_dim.4), calls=%async_computation | async-start | bytes 196608 | tf_op jit(solution)/shard_map/all_to_all | solution.py:234
  17.3 0.0 copy-start.3
  17.4 1.9 %copy-done.3 = bf16[1,1,8,1600,128]{4,3,2,1,0:T(8,128)(2,1)S(1)} copy-done((bf16[1,1,8,1600,128]{4,3,2,1,0:T(8,128)(2,1)S(1)}, bf16[1,1,8,1600,128]{4,3,2,1,0:T(8,128)(2,1)}, u32[]{:S(2)}) %copy-start.3) | copy-done | bytes 3276824
  19.3 0.0 copy-start.7
  19.3 0.0 copy-start.8
  19.3 3.1 %turn_tiles.1.turned_ref = bf16[2,1024,800]{2,1,0:T(8,128)(2,1)S(1)} custom-call(bf16[8,1600,128]{2,1,0:T(8,128)(2,1)S(1)} %bitcast.14), custom_call_target="tpu_custom_call" | custom-call | bytes 6553600 | tf_op jit(solution)/shard_map/turn_tiles/pallas_call | solution.py:45
  22.4 0.0 copy-start.1
  22.4 1.8 %copy-done.1 = bf16[2,1024,800]{2,1,0:T(8,128)(2,1)} copy-done((bf16[2,1024,800]{2,1,0:T(8,128)(2,1)}, bf16[2,1024,800]{2,1,0:T(8,128)(2,1)S(1)}, u32[]{:S(2)}) %copy-start.1) | copy-done | bytes 3276824
  24.2 0.0 copy-start
  24.2 0.0 copy-done.7
  24.2 0.0 copy-done.8
  24.2 0.1 pad_add_fusion.meta_ref
  24.3 2.6 %all-to-all-done.probes_ref = bf16[24,12,128]{2,1,0:T(8,128)(2,1)S(1)} async-done(((bf16[24,12,128]{2,1,0:T(8,128)(2,1)}), bf16[24,12,128]{2,1,0:T(8,128)(2,1)S(1)}, u32[]{:S(2)}, u32[]{:S(2)}) %all-to-all-start) | async-done | bytes 73760 | tf_op jit(solution)/shard_map/all_to_all | solution.py:234
  26.9 0.0 copy-start.2
  26.9 2.0 %copy-done.2 = bf16[2,1024,800]{2,1,0:T(8,128)(2,1)S(1)} copy-done((bf16[2,1024,800]{2,1,0:T(8,128)(2,1)S(1)}, bf16[2,1024,800]{2,1,0:T(8,128)(2,1)}, u32[]{:S(2)}) %copy-start.2) | copy-done | bytes 3276824
  28.9 2.0 %u_blocks.1 = bf16[24,8,896]{2,1,0:T(8,128)(2,1)} custom-call(s32[17]{0:T(128)S(1)} %pad_add_fusion.meta_ref, bf16[24,12,128]{2,1,0:T(8,128)(2,1)S(1)} %all-to-all-done.probes_ref, bf16[2,1024,800]{2,1,0:T(8,128)(2,1)S(1)} %copy-done.2), custom_call_target="tpu_custom_call" | custom-call | tf_op jit(solution)/shard_map/u_blocks/pallas_call | solution.py:87
  31.0 7.6 %all-to-all-start.1 = ((bf16[24,8,896]{2,1,0:T(8,128)(2,1)}), bf16[24,8,896]{2,1,0:T(8,128)(2,1)S(1)}, u32[]{:S(2)}, u32[]{:S(2)}) async-start(bf16[24,8,896]{2,1,0:T(8,128)(2,1)} %u_blocks.1), calls=%async_computation.1 | async-start | bytes 688128 | tf_op jit(solution)/shard_map/all_to_all | solution.py:256
  38.5 0.0 copy-done
  38.5 0.1 slice_bitcast_fusion
  38.7 3.4 %collective-permute-start = (bf16[320,1280]{1,0:T(8,128)(2,1)S(1)}, bf16[320,1280]{1,0:T(8,128)(2,1)S(1)}, u32[]{:S(2)}, u32[]{:S(2)}) collective-permute-start(bf16[320,1280]{1,0:T(8,128)(2,1)S(1)} %get-tuple-element.12), channel_id=1, source_target_pairs={{0,8},{8,0},{1,9},{9,1},{2,10},{10,2},{3,11},{11,3},{4,12},{12,4},... | collective-permute-start | bytes 2457608 | tf_op jit(solution)/shard_map/ppermute | solution.py:244
  42.1 1.9 %collective-permute-start.1 = (bf16[320,1280]{1,0:T(8,128)(2,1)S(1)}, bf16[320,1280]{1,0:T(8,128)(2,1)S(1)}, u32[]{:S(2)}, u32[]{:S(2)}) collective-permute-start(bf16[320,1280]{1,0:T(8,128)(2,1)S(1)} %get-tuple-element.11), channel_id=1, source_target_pairs={{0,8},{8,0},{1,9},{9,1},{2,10},{10,2},{3,11},{11,3},{4,12},{12,4},... | collective-permute-start | bytes 2457608 | tf_op jit(solution)/shard_map/ppermute | solution.py:244
  44.0 0.0 collective-permute-done.vir_ref
  44.0 2.3 %collective-permute-done.1.occ_ref = bf16[320,1280]{1,0:T(8,128)(2,1)S(1)} collective-permute-done((bf16[320,1280]{1,0:T(8,128)(2,1)S(1)}, bf16[320,1280]{1,0:T(8,128)(2,1)S(1)}, u32[]{:S(2)}, u32[]{:S(2)}) %collective-permute-start.1) | collective-permute-done | bytes 819232 | tf_op jit(solution)/shard_map/ppermute | solution.py:244
  46.3 0.0 copy-start.5
  46.3 0.9 copy-done.5
  47.2 7.5 %all-to-all-done.1.recv_ref = bf16[24,8,896]{2,1,0:T(8,128)(2,1)S(1)} async-done(((bf16[24,8,896]{2,1,0:T(8,128)(2,1)}), bf16[24,8,896]{2,1,0:T(8,128)(2,1)S(1)}, u32[]{:S(2)}, u32[]{:S(2)}) %all-to-all-start.1) | async-done | bytes 344096 | tf_op jit(solution)/shard_map/all_to_all | solution.py:256
  54.7 1.0 u_by_atom.1
  55.7 7.7 %collective-permute-start.2 = (bf16[20,1280]{1,0:T(8,128)(2,1)S(1)}, bf16[20,1280]{1,0:T(8,128)(2,1)S(1)}, u32[]{:S(2)}, u32[]{:S(2)}) collective-permute-start(bf16[20,1280]{1,0:T(8,128)(2,1)S(1)} %u_by_atom.1), channel_id=1, source_target_pairs={{0,400},{16,384},{128,528},{144,512},{256,656},{272,640},{384,16},... | collective-permute-start | bytes 153608 | tf_op jit(solution)/shard_map/ppermute | solution.py:240
  63.4 1.8 %collective-permute-done.2.rows_ref = bf16[20,1280]{1,0:T(8,128)(2,1)S(1)} collective-permute-done((bf16[20,1280]{1,0:T(8,128)(2,1)S(1)}, bf16[20,1280]{1,0:T(8,128)(2,1)S(1)}, u32[]{:S(2)}, u32[]{:S(2)}) %collective-permute-start.2) | collective-permute-done | bytes 51232 | tf_op jit(solution)/shard_map/ppermute | solution.py:240
  65.2 0.0 copy-start.6
  65.2 1.1 copy-done.6
  66.4 0.9 v_far.1
  67.2 0.0 copy-start.4
  67.2 7.1 %collective-permute-start.3 = (bf16[20,1280]{1,0:T(8,128)(2,1)S(1)}, bf16[20,1280]{1,0:T(8,128)(2,1)S(1)}, u32[]{:S(2)}, u32[]{:S(2)}) collective-permute-start(bf16[20,1280]{1,0:T(8,128)(2,1)S(1)} %v_far.1), channel_id=1, source_target_pairs={{0,400},{16,384},{128,528},{144,512},{256,656},{272,640},{384,16},... | collective-permute-start | bytes 153608 | tf_op jit(solution)/shard_map/ppermute | solution.py:240
  74.3 2.2 %v_near.1.near_ref = f32[20,1280]{1,0:T(8,128)S(1)} custom-call(bf16[24,8,896]{2,1,0:T(8,128)(2,1)S(1)} %all-to-all-done.1.recv_ref, bf16[2,320,1280]{2,1,0:T(8,128)(2,1)S(1)} %bitcast.13, bf16[320,1280]{1,0:T(8,128)(2,1)S(1)} %copy-done.6, bf16[320,1280]{1,0:T(8,128)(2,1)S(1)} %collective-permute-done.vir_ref), custom_call_target="tpu_custom_call" | custom-call | tf_op jit(solution)/shard_map/v_near/pallas_call | solution.py:167
  76.5 0.0 collective-permute-done.3.far_ref
  76.5 1.0 v_back.1
  77.5 20.2 %all_to_all.25.v_ref = bf16[24,8,800]{2,1,0:T(8,128)(2,1)S(1)} all-to-all(bf16[24,8,800]{2,1,0:T(8,128)(2,1)S(1)} %v_back.1), channel_id=1, replica_groups=mesh['z_lo'=6,'x'=4,'z_hi'=2,'core'=2,'rep'=8] {'z_lo','x'}, dimensions={0} | all-to-all | bytes 614400 | tf_op jit(solution)/shard_map/all_to_all | solution.py:260
  97.7 0.0 copy-done.4
  97.7 1.4 y_by_owner.1
  99.1 20.5 %all_to_all.26 = bf16[48,12,128]{2,1,0:T(8,128)(2,1)S(1)} all-to-all(bf16[48,12,128]{2,1,0:T(8,128)(2,1)S(1)} %bitcast.16), channel_id=1, replica_groups=mesh['z_lo'=6,'x'=4,'z_hi'=2,'core'=2,'rep'=8] {'z_hi','z_lo','x'}, dimensions={0} | all-to-all | bytes 294912 | tf_op jit(solution)/shard_map/all_to_all | solution.py:261
  119.5 0.1 reduce_sum.21
  119.6 21.0 %all_to_all.27 = bf16[16,12,128]{2,1,0:T(8,128)(2,1)S(1)} all-to-all(bf16[16,12,128]{2,1,0:T(8,128)(2,1)S(1)} %broadcast_in_dim.5), channel_id=1, replica_groups=mesh['z_lo'=6,'x'=4,'z_hi'=2,'core'=2,'rep'=8] {'core','rep'}, dimensions={0} | all-to-all | bytes 98304 | tf_op jit(solution)/shard_map/all_to_all | solution.py:234
  140.6 0.6 convert_reduce_fusion
  (1 shorter events, 0.0 us)
Async XLA Ops:
  1.3 25.5 %all-to-all-start = ((bf16[24,12,128]{2,1,0:T(8,128)(2,1)}), bf16[24,12,128]{2,1,0:T(8,128)(2,1)S(1)}, u32[]{:S(2)}, u32[]{:S(2)}) async-start(bf16[24,12,128]{2,1,0:T(8,128)(2,1)} %broadcast_in_dim.4), calls=%async_computation | async-start | bytes 196608 | tf_op jit(solution)/shard_map/all_to_all | solution.py:234
  17.3 1.9 %copy-start.3 = (bf16[1,1,8,1600,128]{4,3,2,1,0:T(8,128)(2,1)S(1)}, bf16[1,1,8,1600,128]{4,3,2,1,0:T(8,128)(2,1)}, u32[]{:S(2)}) copy-start(bf16[1,1,8,1600,128]{4,3,2,1,0:T(8,128)(2,1)} %param.6) | copy-start | bytes 9830404
  19.3 4.9 %copy-start.7 = (s32[1,1,8]{2,1,0:T(1,128)S(1)}, s32[1,1,8]{2,1,0:T(1,128)}, u32[]{:S(2)}) copy-start(s32[1,1,8]{2,1,0:T(1,128)} %param.7) | copy-start | bytes 100
  19.3 4.9 %copy-start.8 = (s32[1,1,8]{2,1,0:T(1,128)S(1)}, s32[1,1,8]{2,1,0:T(1,128)}, u32[]{:S(2)}) copy-start(s32[1,1,8]{2,1,0:T(1,128)} %param.8) | copy-start | bytes 100
  22.4 1.8 %copy-start.1 = (bf16[2,1024,800]{2,1,0:T(8,128)(2,1)}, bf16[2,1024,800]{2,1,0:T(8,128)(2,1)S(1)}, u32[]{:S(2)}) copy-start(bf16[2,1024,800]{2,1,0:T(8,128)(2,1)S(1)} %turn_tiles.1.turned_ref) | copy-start | bytes 9830404
  24.2 14.3 %copy-start = (bf16[2,1280,320]{1,2,0:T(8,128)(2,1)S(1)}, bf16[2,1280,320]{1,2,0:T(8,128)(2,1)}, u32[]{:S(2)}) copy-start(bf16[2,1280,320]{1,2,0:T(8,128)(2,1)} %param.10) | copy-start | bytes 4915204
  26.9 2.0 %copy-start.2 = (bf16[2,1024,800]{2,1,0:T(8,128)(2,1)S(1)}, bf16[2,1024,800]{2,1,0:T(8,128)(2,1)}, u32[]{:S(2)}) copy-start(bf16[2,1024,800]{2,1,0:T(8,128)(2,1)} %copy-done.1) | copy-start | bytes 9830404
  31.0 23.8 %all-to-all-start.1 = ((bf16[24,8,896]{2,1,0:T(8,128)(2,1)}), bf16[24,8,896]{2,1,0:T(8,128)(2,1)S(1)}, u32[]{:S(2)}, u32[]{:S(2)}) async-start(bf16[24,8,896]{2,1,0:T(8,128)(2,1)} %u_blocks.1), calls=%async_computation.1 | async-start | bytes 688128 | tf_op jit(solution)/shard_map/all_to_all | solution.py:256
  38.7 5.4 %collective-permute-start = (bf16[320,1280]{1,0:T(8,128)(2,1)S(1)}, bf16[320,1280]{1,0:T(8,128)(2,1)S(1)}, u32[]{:S(2)}, u32[]{:S(2)}) collective-permute-start(bf16[320,1280]{1,0:T(8,128)(2,1)S(1)} %get-tuple-element.12), channel_id=1, source_target_pairs={{0,8},{8,0},{1,9},{9,1},{2,10},{10,2},{3,11},{11,3},{4,12},{12,4},... | collective-permute-start | bytes 2457608 | tf_op jit(solution)/shard_map/ppermute | solution.py:244
  42.1 4.2 %collective-permute-start.1 = (bf16[320,1280]{1,0:T(8,128)(2,1)S(1)}, bf16[320,1280]{1,0:T(8,128)(2,1)S(1)}, u32[]{:S(2)}, u32[]{:S(2)}) collective-permute-start(bf16[320,1280]{1,0:T(8,128)(2,1)S(1)} %get-tuple-element.11), channel_id=1, source_target_pairs={{0,8},{8,0},{1,9},{9,1},{2,10},{10,2},{3,11},{11,3},{4,12},{12,4},... | collective-permute-start | bytes 2457608 | tf_op jit(solution)/shard_map/ppermute | solution.py:244
  46.3 0.9 copy-start.5
  55.7 9.5 %collective-permute-start.2 = (bf16[20,1280]{1,0:T(8,128)(2,1)S(1)}, bf16[20,1280]{1,0:T(8,128)(2,1)S(1)}, u32[]{:S(2)}, u32[]{:S(2)}) collective-permute-start(bf16[20,1280]{1,0:T(8,128)(2,1)S(1)} %u_by_atom.1), channel_id=1, source_target_pairs={{0,400},{16,384},{128,528},{144,512},{256,656},{272,640},{384,16},... | collective-permute-start | bytes 153608 | tf_op jit(solution)/shard_map/ppermute | solution.py:240
  65.2 1.1 copy-start.6
  67.2 30.5 %copy-start.4 = (bf16[1,1,8,1600,128]{4,3,2,1,0:T(8,128)(2,1)S(1)}, bf16[1,1,8,1600,128]{4,3,2,1,0:T(8,128)(2,1)}, u32[]{:S(2)}) copy-start(bf16[1,1,8,1600,128]{4,3,2,1,0:T(8,128)(2,1)} %param.6) | copy-start | bytes 9830404
  67.2 9.3 %collective-permute-start.3 = (bf16[20,1280]{1,0:T(8,128)(2,1)S(1)}, bf16[20,1280]{1,0:T(8,128)(2,1)S(1)}, u32[]{:S(2)}, u32[]{:S(2)}) collective-permute-start(bf16[20,1280]{1,0:T(8,128)(2,1)S(1)} %v_far.1), channel_id=1, source_target_pairs={{0,400},{16,384},{128,528},{144,512},{256,656},{272,640},{384,16},... | collective-permute-start | bytes 153608 | tf_op jit(solution)/shard_map/ppermute | solution.py:240

commit v7 on v6

--- a/solution.py
+++ b/solution.py
@@ -250,10 +250,11 @@
     groups = lax.axis_size(AUX)
     meta = jnp.concatenate([owner_of[0, 0], atom_of[0, 0], live_count[0]])
     mine = jnp.swapaxes(green, 1, 2)
-    vir, occ = swapped(mine[1]), swapped(mine[0])
+    vir = swapped(mine[1])
     probes_all = everywhere(probes, AUX)
     u = make_u(turn(tiles), probes_all, meta, slot_count)
-    u, vir, occ = lax.optimization_barrier((lax.all_to_all(u, AUX, 0, 0), vir, occ))
+    u, vir, own = lax.optimization_barrier((lax.all_to_all(u, AUX, 0, 0), vir, mine[0]))
+    occ = swapped(own)
     near = make_near(u, mine, occ, vir)
     far = beyond(make_far(beyond(make_rows(u, mine.shape[2])), mine, occ, vir))
     v = make_back(u, near, far)

time: 142 us -> 147 us (1.035)
  waiting for transfers between devices: 14.2 us -> 17.4 us
  starting transfers between devices: 43.1 us -> 46.2 us
    all_to_all x1, blocking collectives: 21 us -> 18.3 us  [everywhere(): return lax.all_to_all(copies, axes, 0, 0)]
    all_to_all x1, waiting for transfers between devices: 7.49 us -> 9.82 us  [body(): lax.all_to_all(u, AUX, 0, 0)]
    all_to_all x1, blocking collectives: 20.5 us -> 22.7 us  [body(): y = lax.all_to_all(y.reshape((Z_HI * groups,) + y.shape[2:]), OUTER, 0, 0)]
    ppermute x2, starting transfers between devices: 5.33 us -> 7.6 us  [swapped(): return lax.ppermute(value, 'core', [(0, 1), (1, 0)])]
    unnamed x18 -> x14, local copies, waits for them, and re-layouts: 7.83 us -> 5.77 us
  transfers between devices with their start and end apart: 6 -> 6, of which waited for: 4 -> 5; matrix products, arithmetic and copies ran while one was open for 0% -> 1% of each run, Pallas kernels for 4% -> 4%
where the time goes in v7:
time: 147 us
  blocking collectives  61.9 us (42%)
  starting transfers between devices  46.2 us (31%)
  waiting for transfers between devices  17.4 us (12%)
  Pallas kernels  11.5 us (8%)
  local copies, waits for them, and re-layouts  8.12 us (6%)
    all_to_all x1, blocking collectives, body(): y = lax.all_to_all(y.reshape((Z_HI * groups,) + y.shape[2:]), OUTER, 0, 0)  22.7 us
    all_to_all x1, blocking collectives, body(): y = make_y(lax.all_to_all(v, AUX, 0, 0), tiles, meta, groups)  20.9 us
    all_to_all x1, blocking collectives, everywhere(): return lax.all_to_all(copies, axes, 0, 0)  18.3 us
    ppermute x2, starting transfers between devices, beyond(): return lax.ppermute(value, ('z_lo', 'z_hi'), pairs)  15.7 us
    all_to_all x1, starting transfers between devices, everywhere(): return lax.all_to_all(copies, axes, 0, 0)  15.4 us
    all_to_all x1, waiting for transfers between devices, body(): lax.all_to_all(u, AUX, 0, 0)  9.82 us
    ppermute x2, starting transfers between devices, swapped(): return lax.ppermute(value, 'core', [(0, 1), (1, 0)])  7.6 us
    all_to_all x1, starting transfers between devices, body(): lax.all_to_all(u, AUX, 0, 0)  7.59 us
  transfers between devices with their start and end apart: 6, of which 5 were waited for; matrix products, arithmetic and copies ran while one was open for 1% of the time, Pallas kernels for 4%

profile of v7, /device:TPU:1, one launch (start us, length us, event | category | flops | bytes accessed | tf_op | source)
XLA Modules:
  0.0 146.6 jit_solution(7996208616873279843)
XLA Ops:
  0.0 1.3 broadcast_in_dim.4
  1.3 15.4 %all-to-all-start = ((bf16[24,12,128]{2,1,0:T(8,128)(2,1)}), bf16[24,12,128]{2,1,0:T(8,128)(2,1)S(1)}, u32[]{:S(2)}, u32[]{:S(2)}) async-start(bf16[24,12,128]{2,1,0:T(8,128)(2,1)} %broadcast_in_dim.4), calls=%async_computation | async-start | bytes 196608 | tf_op jit(solution)/shard_map/all_to_all | solution.py:234
  17.3 0.0 copy-start.3
  17.4 1.9 %copy-done.3 = bf16[1,1,8,1600,128]{4,3,2,1,0:T(8,128)(2,1)S(1)} copy-done((bf16[1,1,8,1600,128]{4,3,2,1,0:T(8,128)(2,1)S(1)}, bf16[1,1,8,1600,128]{4,3,2,1,0:T(8,128)(2,1)}, u32[]{:S(2)}) %copy-start.3) | copy-done | bytes 3276824
  19.3 0.0 copy-start.5
  19.3 0.0 copy-start.6
  19.3 3.1 %turn_tiles.1.turned_ref = bf16[2,1024,800]{2,1,0:T(8,128)(2,1)S(1)} custom-call(bf16[8,1600,128]{2,1,0:T(8,128)(2,1)S(1)} %bitcast.14), custom_call_target="tpu_custom_call" | custom-call | bytes 6553600 | tf_op jit(solution)/shard_map/turn_tiles/pallas_call | solution.py:45
  22.4 0.0 copy-start.1
  22.4 1.8 %copy-done.1 = bf16[2,1024,800]{2,1,0:T(8,128)(2,1)} copy-done((bf16[2,1024,800]{2,1,0:T(8,128)(2,1)}, bf16[2,1024,800]{2,1,0:T(8,128)(2,1)S(1)}, u32[]{:S(2)}) %copy-start.1) | copy-done | bytes 3276824
  24.2 0.0 copy-start
  24.2 0.0 copy-done.5
  24.2 0.0 copy-done.6
  24.2 0.1 pad_add_fusion.meta_ref
  24.3 2.6 %all-to-all-done.probes_ref = bf16[24,12,128]{2,1,0:T(8,128)(2,1)S(1)} async-done(((bf16[24,12,128]{2,1,0:T(8,128)(2,1)}), bf16[24,12,128]{2,1,0:T(8,128)(2,1)S(1)}, u32[]{:S(2)}, u32[]{:S(2)}) %all-to-all-start) | async-done | bytes 73760 | tf_op jit(solution)/shard_map/all_to_all | solution.py:234
  26.9 0.0 copy-start.2
  26.9 2.0 %copy-done.2 = bf16[2,1024,800]{2,1,0:T(8,128)(2,1)S(1)} copy-done((bf16[2,1024,800]{2,1,0:T(8,128)(2,1)S(1)}, bf16[2,1024,800]{2,1,0:T(8,128)(2,1)}, u32[]{:S(2)}) %copy-start.2) | copy-done | bytes 3276824
  28.9 2.0 %u_blocks.1 = bf16[24,8,896]{2,1,0:T(8,128)(2,1)} custom-call(s32[17]{0:T(128)S(1)} %pad_add_fusion.meta_ref, bf16[24,12,128]{2,1,0:T(8,128)(2,1)S(1)} %all-to-all-done.probes_ref, bf16[2,1024,800]{2,1,0:T(8,128)(2,1)S(1)} %copy-done.2), custom_call_target="tpu_custom_call" | custom-call | tf_op jit(solution)/shard_map/u_blocks/pallas_call | solution.py:87
  30.9 7.6 %all-to-all-start.1 = ((bf16[24,8,896]{2,1,0:T(8,128)(2,1)}), bf16[24,8,896]{2,1,0:T(8,128)(2,1)S(1)}, u32[]{:S(2)}, u32[]{:S(2)}) async-start(bf16[24,8,896]{2,1,0:T(8,128)(2,1)} %u_blocks.1), calls=%async_computation.1 | async-start | bytes 688128 | tf_op jit(solution)/shard_map/all_to_all | solution.py:256
  38.5 0.0 copy-done
  38.6 1.0 slice_bitcast_fusion
  39.6 3.4 %collective-permute-start = (bf16[320,1280]{1,0:T(8,128)(2,1)S(1)}, bf16[320,1280]{1,0:T(8,128)(2,1)S(1)}, u32[]{:S(2)}, u32[]{:S(2)}) collective-permute-start(bf16[320,1280]{1,0:T(8,128)(2,1)S(1)} %get-tuple-element.12), channel_id=1, source_target_pairs={{0,8},{8,0},{1,9},{9,1},{2,10},{10,2},{3,11},{11,3},{4,12},{12,4},... | collective-permute-start | bytes 2457608 | tf_op jit(solution)/shard_map/ppermute | solution.py:244
  43.0 1.9 %collective-permute-done.vir_ref = bf16[320,1280]{1,0:T(8,128)(2,1)S(1)} collective-permute-done((bf16[320,1280]{1,0:T(8,128)(2,1)S(1)}, bf16[320,1280]{1,0:T(8,128)(2,1)S(1)}, u32[]{:S(2)}, u32[]{:S(2)}) %collective-permute-start) | collective-permute-done | bytes 819232 | tf_op jit(solution)/shard_map/ppermute | solution.py:244
  44.9 9.8 %all-to-all-done.1.recv_ref = bf16[24,8,896]{2,1,0:T(8,128)(2,1)S(1)} async-done(((bf16[24,8,896]{2,1,0:T(8,128)(2,1)}), bf16[24,8,896]{2,1,0:T(8,128)(2,1)S(1)}, u32[]{:S(2)}, u32[]{:S(2)}) %all-to-all-start.1) | async-done | bytes 344096 | tf_op jit(solution)/shard_map/all_to_all | solution.py:256
  54.7 4.2 %collective-permute-start.1 = (bf16[320,1280]{1,0:T(8,128)(2,1)}, bf16[320,1280]{1,0:T(8,128)(2,1)S(1)}, u32[]{:S(2)}, u32[]{:S(2)}) collective-permute-start(bf16[320,1280]{1,0:T(8,128)(2,1)} %get-tuple-element.9), channel_id=1, source_target_pairs={{0,8},{8,0},{1,9},{9,1},{2,10},{10,2},{3,11},{11,3},{4,12},{12,4},... | collective-permute-start | bytes 2457608 | tf_op jit(solution)/shard_map/ppermute | solution.py:244
  58.9 1.0 u_by_atom.1
  59.9 6.6 %collective-permute-start.2 = (bf16[20,1280]{1,0:T(8,128)(2,1)S(1)}, bf16[20,1280]{1,0:T(8,128)(2,1)S(1)}, u32[]{:S(2)}, u32[]{:S(2)}) collective-permute-start(bf16[20,1280]{1,0:T(8,128)(2,1)S(1)} %u_by_atom.1), channel_id=1, source_target_pairs={{0,400},{16,384},{128,528},{144,512},{256,656},{272,640},{384,16},... | collective-permute-start | bytes 153608 | tf_op jit(solution)/shard_map/ppermute | solution.py:240
  66.5 2.4 %collective-permute-done.2.rows_ref = bf16[20,1280]{1,0:T(8,128)(2,1)S(1)} collective-permute-done((bf16[20,1280]{1,0:T(8,128)(2,1)S(1)}, bf16[20,1280]{1,0:T(8,128)(2,1)S(1)}, u32[]{:S(2)}, u32[]{:S(2)}) %collective-permute-start.2) | collective-permute-done | bytes 51232 | tf_op jit(solution)/shard_map/ppermute | solution.py:240
  68.9 0.0 collective-permute-done.1.occ_ref
  68.9 0.9 v_far.1
  69.8 0.0 copy-start.4
  69.8 9.0 %collective-permute-start.3 = (bf16[20,1280]{1,0:T(8,128)(2,1)S(1)}, bf16[20,1280]{1,0:T(8,128)(2,1)S(1)}, u32[]{:S(2)}, u32[]{:S(2)}) collective-permute-start(bf16[20,1280]{1,0:T(8,128)(2,1)S(1)} %v_far.1), channel_id=1, source_target_pairs={{0,400},{16,384},{128,528},{144,512},{256,656},{272,640},{384,16},... | collective-permute-start | bytes 153608 | tf_op jit(solution)/shard_map/ppermute | solution.py:240
  78.8 2.2 %v_near.1.near_ref = f32[20,1280]{1,0:T(8,128)S(1)} custom-call(bf16[24,8,896]{2,1,0:T(8,128)(2,1)S(1)} %all-to-all-done.1.recv_ref, bf16[2,320,1280]{2,1,0:T(8,128)(2,1)S(1)} %bitcast.13, bf16[320,1280]{1,0:T(8,128)(2,1)S(1)} %collective-permute-done.1.occ_ref, bf16[320,1280]{1,0:T(8,128)(2,1)S(1)} %collective-permute-done.vir_ref), custom_call_target="tpu_custom_call" | custom-call | tf_op jit(solution)/shard_map/v_near/pallas_call | solution.py:167
  81.0 0.7 collective-permute-done.3.far_ref
  81.7 0.9 v_back.1
  82.7 20.9 %all_to_all.25.v_ref = bf16[24,8,800]{2,1,0:T(8,128)(2,1)S(1)} all-to-all(bf16[24,8,800]{2,1,0:T(8,128)(2,1)S(1)} %v_back.1), channel_id=1, replica_groups=mesh['z_lo'=6,'x'=4,'z_hi'=2,'core'=2,'rep'=8] {'z_lo','x'}, dimensions={0} | all-to-all | bytes 614400 | tf_op jit(solution)/shard_map/all_to_all | solution.py:261
  103.5 0.0 copy-done.4
  103.5 1.4 y_by_owner.1
  104.9 22.7 %all_to_all.26 = bf16[48,12,128]{2,1,0:T(8,128)(2,1)S(1)} all-to-all(bf16[48,12,128]{2,1,0:T(8,128)(2,1)S(1)} %bitcast.16), channel_id=1, replica_groups=mesh['z_lo'=6,'x'=4,'z_hi'=2,'core'=2,'rep'=8] {'z_hi','z_lo','x'}, dimensions={0} | all-to-all | bytes 294912 | tf_op jit(solution)/shard_map/all_to_all | solution.py:262
  127.6 0.1 reduce_sum.21
  127.7 18.3 %all_to_all.27 = bf16[16,12,128]{2,1,0:T(8,128)(2,1)S(1)} all-to-all(bf16[16,12,128]{2,1,0:T(8,128)(2,1)S(1)} %broadcast_in_dim.5), channel_id=1, replica_groups=mesh['z_lo'=6,'x'=4,'z_hi'=2,'core'=2,'rep'=8] {'core','rep'}, dimensions={0} | all-to-all | bytes 98304 | tf_op jit(solution)/shard_map/all_to_all | solution.py:234
  146.0 0.6 convert_reduce_fusion
  (1 shorter events, 0.0 us)
Async XLA Ops:
  1.3 25.5 %all-to-all-start = ((bf16[24,12,128]{2,1,0:T(8,128)(2,1)}), bf16[24,12,128]{2,1,0:T(8,128)(2,1)S(1)}, u32[]{:S(2)}, u32[]{:S(2)}) async-start(bf16[24,12,128]{2,1,0:T(8,128)(2,1)} %broadcast_in_dim.4), calls=%async_computation | async-start | bytes 196608 | tf_op jit(solution)/shard_map/all_to_all | solution.py:234
  17.3 1.9 %copy-start.3 = (bf16[1,1,8,1600,128]{4,3,2,1,0:T(8,128)(2,1)S(1)}, bf16[1,1,8,1600,128]{4,3,2,1,0:T(8,128)(2,1)}, u32[]{:S(2)}) copy-start(bf16[1,1,8,1600,128]{4,3,2,1,0:T(8,128)(2,1)} %param.6) | copy-start | bytes 9830404
  19.3 5.0 %copy-start.5 = (s32[1,1,8]{2,1,0:T(1,128)S(1)}, s32[1,1,8]{2,1,0:T(1,128)}, u32[]{:S(2)}) copy-start(s32[1,1,8]{2,1,0:T(1,128)} %param.7) | copy-start | bytes 100
  19.3 5.0 %copy-start.6 = (s32[1,1,8]{2,1,0:T(1,128)S(1)}, s32[1,1,8]{2,1,0:T(1,128)}, u32[]{:S(2)}) copy-start(s32[1,1,8]{2,1,0:T(1,128)} %param.8) | copy-start | bytes 100
  22.4 1.8 %copy-start.1 = (bf16[2,1024,800]{2,1,0:T(8,128)(2,1)}, bf16[2,1024,800]{2,1,0:T(8,128)(2,1)S(1)}, u32[]{:S(2)}) copy-start(bf16[2,1024,800]{2,1,0:T(8,128)(2,1)S(1)} %turn_tiles.1.turned_ref) | copy-start | bytes 9830404
  24.2 14.3 %copy-start = (bf16[2,1280,320]{1,2,0:T(8,128)(2,1)S(1)}, bf16[2,1280,320]{1,2,0:T(8,128)(2,1)}, u32[]{:S(2)}) copy-start(bf16[2,1280,320]{1,2,0:T(8,128)(2,1)} %param.10) | copy-start | bytes 4915204
  26.9 2.0 %copy-start.2 = (bf16[2,1024,800]{2,1,0:T(8,128)(2,1)S(1)}, bf16[2,1024,800]{2,1,0:T(8,128)(2,1)}, u32[]{:S(2)}) copy-start(bf16[2,1024,800]{2,1,0:T(8,128)(2,1)} %copy-done.1) | copy-start | bytes 9830404
  30.9 23.8 %all-to-all-start.1 = ((bf16[24,8,896]{2,1,0:T(8,128)(2,1)}), bf16[24,8,896]{2,1,0:T(8,128)(2,1)S(1)}, u32[]{:S(2)}, u32[]{:S(2)}) async-start(bf16[24,8,896]{2,1,0:T(8,128)(2,1)} %u_blocks.1), calls=%async_computation.1 | async-start | bytes 688128 | tf_op jit(solution)/shard_map/all_to_all | solution.py:256
  39.6 5.3 %collective-permute-start = (bf16[320,1280]{1,0:T(8,128)(2,1)S(1)}, bf16[320,1280]{1,0:T(8,128)(2,1)S(1)}, u32[]{:S(2)}, u32[]{:S(2)}) collective-permute-start(bf16[320,1280]{1,0:T(8,128)(2,1)S(1)} %get-tuple-element.12), channel_id=1, source_target_pairs={{0,8},{8,0},{1,9},{9,1},{2,10},{10,2},{3,11},{11,3},{4,12},{12,4},... | collective-permute-start | bytes 2457608 | tf_op jit(solution)/shard_map/ppermute | solution.py:244
  54.7 14.2 %collective-permute-start.1 = (bf16[320,1280]{1,0:T(8,128)(2,1)}, bf16[320,1280]{1,0:T(8,128)(2,1)S(1)}, u32[]{:S(2)}, u32[]{:S(2)}) collective-permute-start(bf16[320,1280]{1,0:T(8,128)(2,1)} %get-tuple-element.9), channel_id=1, source_target_pairs={{0,8},{8,0},{1,9},{9,1},{2,10},{10,2},{3,11},{11,3},{4,12},{12,4},... | collective-permute-start | bytes 2457608 | tf_op jit(solution)/shard_map/ppermute | solution.py:244
  59.9 9.0 %collective-permute-start.2 = (bf16[20,1280]{1,0:T(8,128)(2,1)S(1)}, bf16[20,1280]{1,0:T(8,128)(2,1)S(1)}, u32[]{:S(2)}, u32[]{:S(2)}) collective-permute-start(bf16[20,1280]{1,0:T(8,128)(2,1)S(1)} %u_by_atom.1), channel_id=1, source_target_pairs={{0,400},{16,384},{128,528},{144,512},{256,656},{272,640},{384,16},... | collective-permute-start | bytes 153608 | tf_op jit(solution)/shard_map/ppermute | solution.py:240
  69.8 33.7 %copy-start.4 = (bf16[1,1,8,1600,128]{4,3,2,1,0:T(8,128)(2,1)S(1)}, bf16[1,1,8,1600,128]{4,3,2,1,0:T(8,128)(2,1)}, u32[]{:S(2)}) copy-start(bf16[1,1,8,1600,128]{4,3,2,1,0:T(8,128)(2,1)} %param.6) | copy-start | bytes 9830404
  69.8 11.9 %collective-permute-start.3 = (bf16[20,1280]{1,0:T(8,128)(2,1)S(1)}, bf16[20,1280]{1,0:T(8,128)(2,1)S(1)}, u32[]{:S(2)}, u32[]{:S(2)}) collective-permute-start(bf16[20,1280]{1,0:T(8,128)(2,1)S(1)} %v_far.1), channel_id=1, source_target_pairs={{0,400},{16,384},{128,528},{144,512},{256,656},{272,640},{384,16},... | collective-permute-start | bytes 153608 | tf_op jit(solution)/shard_map/ppermute | solution.py:240
